TPU v7x, 32 devices: a whole 2x2x4 slice. The times are simulated.
32 devices in a mesh: lat: 4 (over y, x), lon: 8 (over z, core).
Axes of the slice: x: 2, y: 2, z: 4, core: 2. Of those that a mesh axis runs over, the one named last changes fastest.
Arguments:
- latent_state: bfloat16 [2, 96, 192, 1024], P(None, 'lat', 'lon'), may hold values from -6 to 6
- obs_rows: bfloat16 [4, 8, 1024, 256], P('lat', 'lon'), may hold values from -6 to 6
- obs_cells: int32 [4, 8, 1024], P('lat', 'lon'), may hold values from 0 to 1151
- obs_counts: int32 [4, 8, 32], P('lat', 'lon'), may hold values from 0 to 32, as said below
- w_obs: bfloat16 [256, 1024], replicated, may hold values from -0.375 to 0.375
- w_qkv: bfloat16 [1024, 3072], replicated, may hold values from -0.1875 to 0.1875
- w_out: bfloat16 [1024, 1024], replicated, may hold values from -0.1875 to 0.1875
- logit_scale: float32 [16], replicated, may hold values from 3 to 24
- pos_bias: float32 [16, 144, 144], replicated, may hold values from -4 to 4
- out_gain: float32 [1024], replicated, may hold values from 0.25 to 1.75
Outputs:
- shifted: bfloat16 [2, 96, 192, 1024], P(None, 'lat', 'lon')
Inputs may be any that keep to these rules, and one draw needn't show every extreme that they name: `obs_counts`: at most 32 live slots from one source for one destination; in every draw some destination gets 32 live slots from every source. `obs_cells`: cells of a device are numbered level, latitude, longitude.
All inputs are finite; a program needn't handle non-finite values.
Results may differ from a plain program's by a relative error of at most 0.0066.
Values may be sent and summed in bfloat16 or wider, within the bound.
No kernel may reach another device: no remote copies, remote signals or barrier semaphores. Data moves between devices by JAX's collectives and lax.ppermute only.
A program may use at most 192 MiB of HBM per device.

v0:
```python
import functools
import math

import jax
import jax.numpy as jnp
from jax import lax
from jax.experimental import pallas as pl
from jax.experimental.pallas import tpu as pltpu
from jax.sharding import PartitionSpec as P

WL = 2
WA = 12
WO = 6
CELLS = WL * WA * WO
HALF_A = WA // 2
HALF_O = WO // 2
GROUP = 256
EXTRA = 8
BLOCK = 32
DIGIT = 32
DEAD = 255
EDGE = 48

cosine_eps = 1e-06
layer_eps = 1e-05
LOG2E = math.log2(math.e)
MIB = 1024 * 1024
LANES = 128

F32 = jnp.float32
BF16 = jnp.bfloat16


def divided(x, n):
    quotient = lax.div(x, jnp.full_like(x, n))
    return quotient, x - quotient * n


def window_parts(row):
    window, inner = divided(row, CELLS)
    level, inner = divided(inner, WA * WO)
    lat, lon = divided(inner, WO)
    return window, level, lat, lon


def dot(a, b):
    return jnp.dot(a, b, preferred_element_type=F32)


def selection(rows, columns):
    return (rows == columns).astype(F32).astype(BF16)


def pack_kernel(rows_ref, cells_ref, counts_ref, packed_ref):
    devices, capacity, channels = rows_ref.shape
    slots = devices * capacity
    for at in range(channels // LANES):
        part = rows_ref[:, :, at * LANES : (at + 1) * LANES]
        packed_ref[:, at * capacity : (at + 1) * capacity] = part
    cells = cells_ref[...]
    high = lax.div(cells, jnp.full_like(cells, DIGIT))
    low = cells - high * DIGIT
    slot = lax.broadcasted_iota(jnp.int32, (1, slots), 1)
    device = lax.broadcasted_iota(jnp.int32, (devices, 1), 0)
    place = lax.broadcasted_iota(jnp.int32, (slots, 1), 0)
    place = lax.rem(place, jnp.full_like(place, capacity))
    lane = lax.broadcasted_iota(jnp.int32, (1, LANES), 1)
    own = divided(slot, capacity)[0] == device
    digits = jnp.zeros((devices, LANES), F32)
    for i, digit in enumerate((high, low)):
        spread = jnp.where(own, digit.astype(F32), 0.0).astype(BF16)
        digits += dot(spread, selection(place + i * capacity, lane))
    same = device == lax.broadcasted_iota(jnp.int32, (1, devices), 1)
    count = jnp.sum(jnp.where(same, counts_ref[...].astype(F32), 0.0), -1, keepdims=True)
    dead = (lane < capacity) & (lane.astype(F32) >= count)
    digits = jnp.where(dead, float(DEAD), digits)
    packed_ref[:, channels // LANES * capacity :] = jnp.broadcast_to(
        digits[:, None, :], (devices, EXTRA, LANES)
    ).astype(BF16)


def pack(rows, cells, counts):
    devices, capacity, channels = rows.shape
    held = channels // LANES * capacity + EXTRA
    return pl.pallas_call(
        pack_kernel,
        out_shape=jax.ShapeDtypeStruct((devices, held, LANES), BF16),
        compiler_params=pltpu.CompilerParams(vmem_limit_bytes=16 * MIB),
    )(rows, cells, counts)


def project_kernel(
    lon_cells,
    latent_ref,
    w_obs_ref,
    wq_ref,
    wk_ref,
    wv_ref,
    bias_ref,
    base_ref,
    folded_ref,
    ordered_ref,
    scaled_ref,
    left,
):
    rows = latent_ref.shape[0]
    strip = WL * WA * lon_cells
    strips = rows // strip
    part = WA * lon_cells

    @pl.when(pl.program_id(0) == 0)
    def _():
        row = lax.broadcasted_iota(jnp.int32, (strip, 1), 0)
        window, level, lat, lon = window_parts(row)
        source = level * part + lat * lon_cells + window * WO + lon
        perm = selection(source, lax.broadcasted_iota(jnp.int32, (1, strip), 1))
        for s in range(strips):
            cells = jnp.concatenate(
                [
                    latent_ref[l * strips * part + s * part : l * strips * part + (s + 1) * part]
                    for l in range(WL)
                ],
                axis=0,
            )
            moved = dot(perm, cells).astype(BF16)
            left[s * strip : (s + 1) * strip] = moved
            ordered_ref[s * strip : (s + 1) * strip] = moved
        left[rows:] = w_obs_ref[...]

    for i, w_ref in enumerate((wq_ref, wk_ref, wv_ref)):
        result = dot(left[...], w_ref[...])
        base_ref[0, i] = result[:rows]
        folded_ref[0, i] = result[rows:].astype(BF16)
    scaled_ref[...] = bias_ref[...] * LOG2E


def project(latent, w_obs, w_qkv, bias, lon_cells):
    rows, features = latent.shape
    channels = w_obs.shape[0]
    columns = w_qkv.shape[1]
    groups = features // GROUP
    heads = bias.shape[0] // groups
    whole = lambda i: (0, 0)
    once = pl.Buffered(buffer_count=1)
    some_heads = pl.BlockSpec((heads, CELLS, CELLS), lambda i: (i, 0, 0))
    return pl.pallas_call(
        functools.partial(project_kernel, lon_cells),
        grid=(groups,),
        in_specs=[
            pl.BlockSpec((rows, features), whole, pipeline_mode=once),
            pl.BlockSpec((channels, features), whole, pipeline_mode=once),
            pl.BlockSpec((features, GROUP), lambda i: (0, i)),
            pl.BlockSpec((features, GROUP), lambda i: (0, groups + i)),
            pl.BlockSpec((features, GROUP), lambda i: (0, 2 * groups + i)),
            some_heads,
        ],
        out_specs=[
            pl.BlockSpec((1, 3, rows, GROUP), lambda i: (i, 0, 0, 0)),
            pl.BlockSpec((1, 3, channels, GROUP), lambda i: (i, 0, 0, 0)),
            pl.BlockSpec((rows, features), whole),
            some_heads,
        ],
        out_shape=[
            jax.ShapeDtypeStruct((groups, 3, rows, GROUP), F32),
            jax.ShapeDtypeStruct((groups, 3, channels, GROUP), BF16),
            jax.ShapeDtypeStruct((rows, features), BF16),
            jax.ShapeDtypeStruct(bias.shape, F32),
        ],
        scratch_shapes=[pltpu.VMEM((rows + channels, features), BF16)],
        compiler_params=pltpu.CompilerParams(vmem_limit_bytes=32 * MIB),
        cost_estimate=pl.CostEstimate(
            flops=2 * (rows + channels) * features * columns,
            bytes_accessed=4 * rows * columns + 2 * features * columns + 4 * rows * features,
            transcendentals=0,
        ),
    )(latent, w_obs, w_qkv, w_qkv, w_qkv, bias)


def strip_kernel(
    strip_at,
    lon_cells,
    lat_cells,
    passed,
    packed_ref,
    scale_ref,
    gain_ref,
    base_ref,
    folded_ref,
    bias_ref,
    ordered_hbm,
    w_obs_hbm,
    w_out_hbm,
    *rest,
):
    carried_ref = rest[0] if passed else None
    near_ref, far_ref, edge_ref, ordered_ref, w_obs_ref, w_out_ref, gathered, context, sems = rest[
        passed:
    ]
    step = pl.program_id(0)
    strip, features = ordered_ref.shape
    windows = strip // CELLS
    groups = features // GROUP
    heads = bias_ref.shape[0]
    width = GROUP // heads
    devices, held, _ = packed_ref.shape
    channels = w_obs_ref.shape[0]
    cuts = channels // LANES
    capacity = (held - EXTRA) // cuts
    copies = [
        pltpu.make_async_copy(ordered_hbm.at[pl.ds(strip_at * strip, strip)], ordered_ref, sems.at[0]),
        pltpu.make_async_copy(w_obs_hbm, w_obs_ref, sems.at[1]),
        pltpu.make_async_copy(w_out_hbm, w_out_ref, sems.at[2]),
    ]

    @pl.when(step == 0)
    def _():
        for copy in copies:
            copy.start()
        row = lax.broadcasted_iota(jnp.int32, (strip, 1), 0)
        window, level, lat, lon = window_parts(row)
        cell = (level * lat_cells + strip_at * WA + lat) * lon_cells + window * WO + lon
        count = BLOCK * capacity
        slot = lax.broadcasted_iota(jnp.int32, (1, count), 1)
        source, place = divided(slot, capacity)
        lane = lax.broadcasted_iota(jnp.int32, (LANES, 1), 0)
        weigh = jnp.where(lane == place, float(DIGIT), 0.0) + jnp.where(
            lane == place + capacity, 1.0, 0.0
        )
        line = lax.broadcasted_iota(jnp.int32, (BLOCK * EXTRA, 1), 0)
        total = jnp.zeros((strip, channels), F32)
        for at in range(0, devices, BLOCK):
            some = slice(at, at + BLOCK)
            digits = packed_ref[some, cuts * capacity :].reshape(BLOCK * EXTRA, LANES)
            values = dot(digits, weigh.astype(BF16))
            target = jnp.sum(
                jnp.where(line == source * EXTRA, values, 0.0), 0, keepdims=True
            )
            rows = [
                packed_ref[some, c * capacity : (c + 1) * capacity].reshape(count, LANES)
                for c in range(cuts)
            ]
            rows = jnp.concatenate(rows, axis=1)
            total += dot(selection(cell, target.astype(jnp.int32)), rows)
        high = total.astype(BF16)
        gathered[0] = high
        gathered[1] = (total - high.astype(F32)).astype(BF16)

    lane_head = lax.broadcasted_iota(jnp.int32, (1, GROUP), 1) // width
    same_head = selection(lax.broadcasted_iota(jnp.int32, (GROUP, 1), 0) // width, lane_head)
    scale = jnp.zeros((1, GROUP), F32)
    for h in range(heads):
        scale = jnp.where(lane_head == h, scale_ref[step * heads + h] * LOG2E, scale)
    left_half = lax.broadcasted_iota(jnp.int32, (CELLS, 2 * width), 1) < width
    blank = jnp.zeros((width, CELLS), BF16)

    high = gathered[0]
    query, keys, values = (base_ref[0, i] + dot(high, folded_ref[0, i]) for i in range(3))
    query_sum = dot((query * query).astype(BF16), same_head)
    keys_sum = dot((keys * keys).astype(BF16), same_head)
    query_n = (query * (lax.rsqrt(query_sum + cosine_eps) * scale)).astype(BF16)
    keys_n = keys * lax.rsqrt(keys_sum + cosine_eps)

    def scored(w):
        here = slice(w * CELLS, (w + 1) * CELLS)
        keys_t = keys_n[here].T.astype(BF16)
        result = []
        for h in range(heads):
            pair, side = h // 2, h % 2
            lanes = slice(2 * pair * width, 2 * (pair + 1) * width)
            picked = keys_t[h * width : (h + 1) * width]
            picked = jnp.concatenate([blank, picked] if side else [picked, blank], axis=0)
            result.append(dot(query_n[here, lanes], picked))
        return result

    def weighted(w, scores):
        here = slice(w * CELLS, (w + 1) * CELLS)
        expo = [jnp.exp2(scores[h] + bias_ref[h]).astype(BF16) for h in range(heads)]
        sums = []
        for h in range(heads):
            lanes = slice(h // 2 * 2 * width, (h // 2 + 1) * 2 * width)
            mixed = jnp.where(left_half == (h % 2 == 0), values[here, lanes], 1.0).astype(BF16)
            sums.append(dot(expo[h], mixed))
        parts = []
        for a, b in zip(sums[::2], sums[1::2]):
            norm = pltpu.roll(jnp.where(left_half, b, a), width, 1)
            parts.append(jnp.where(left_half, a, b) / norm)
        context[step, here] = jnp.concatenate(parts, axis=1).astype(BF16)

    scores = scored(0)
    for w in range(windows):
        after = scored(w + 1) if w + 1 < windows else None
        weighted(w, scores)
        scores = after

    @pl.when(step == groups - 1)
    def _():
        for copy in copies:
            copy.wait()
        pieces = 2
        size = strip // pieces
        cuts = [slice(at * size, (at + 1) * size) for at in range(pieces)]
        projs = [
            dot(jnp.concatenate([context[g, cut] for g in range(groups)], axis=1), w_out_ref[...])
            for cut in cuts
        ]
        latents = [
            ordered_ref[cut].astype(F32)
            + dot(gathered[0, cut], w_obs_ref[...])
            + dot(gathered[1, cut], w_obs_ref[...])
            for cut in cuts
        ]
        done = []
        for proj, latent in zip(projs, latents):
            center = proj - jnp.mean(proj, -1, keepdims=True)
            spread = jnp.mean(center * center, -1, keepdims=True)
            normed = center * lax.rsqrt(spread + layer_eps) * gain_ref[...]
            done.append((latent + normed).astype(BF16))
        done = jnp.concatenate(done, axis=0)
        row = lax.broadcasted_iota(jnp.int32, (1, strip), 1)
        window, level, lat, lon = window_parts(row)
        level = lax.rem(level + WL // 2, jnp.full_like(level, WL))
        half, lat = divided(lat, HALF_A)
        lon = window * WO + lon
        moved = lax.rem(lon + HALF_O, jnp.full_like(lon, lon_cells))
        place = ((half * WL + level) * HALF_A + lat) * lon_cells + moved
        edge = (level * HALF_A + lat) * HALF_O + moved
        size = WL * HALF_A * lon_cells
        for h, out_ref in enumerate((near_ref, far_ref)):
            index = lax.broadcasted_iota(jnp.int32, (size, 1), 0) + h * size
            out_ref[...] = dot(selection(index, place), done).astype(BF16)
            if h == 0 or passed:
                index = lax.broadcasted_iota(jnp.int32, (EDGE, 1), 0)
                wanted = jnp.where((moved < HALF_O) & (half == h), edge, -1)
                chosen = dot(selection(index, wanted), done).astype(BF16)
                edge_ref[h * EDGE : (h + 1) * EDGE] = chosen
        if passed:
            edge_ref[2 * EDGE :] = carried_ref[...]


def attend_strip(
    strip_at, packed, scale, gain, base, folded, bias, ordered, w_obs, w_out, lat_cells, lon_cells,
    carried=None,
):
    strip = WL * WA * lon_cells
    features = w_out.shape[0]
    groups = features // GROUP
    channels = w_obs.shape[0]
    heads = bias.shape[0] // groups
    passed = carried is not None
    whole = lambda i: (0, 0)
    once = pl.Buffered(buffer_count=1)
    there = pl.BlockSpec(memory_space=pl.ANY)
    half = (strip // 2, features)
    outs = [half, half, (3 * EDGE if passed else EDGE, features)]
    extra = [carried] if passed else []
    return pl.pallas_call(
        functools.partial(strip_kernel, strip_at, lon_cells, lat_cells, passed),
        grid=(groups,),
        in_specs=[
            pl.BlockSpec(packed.shape, lambda i: (0, 0, 0), pipeline_mode=once),
            pl.BlockSpec(memory_space=pltpu.SMEM),
            pl.BlockSpec((1, features), whole),
            pl.BlockSpec((1, 3, strip, GROUP), lambda i: (i, 0, strip_at, 0)),
            pl.BlockSpec((1, 3, channels, GROUP), lambda i: (i, 0, 0, 0)),
            pl.BlockSpec((heads, CELLS, CELLS), lambda i: (i, 0, 0)),
            there,
            there,
            there,
        ]
        + [pl.BlockSpec(part.shape, whole, pipeline_mode=once) for part in extra],
        out_specs=[pl.BlockSpec(shape, whole) for shape in outs],
        out_shape=[jax.ShapeDtypeStruct(shape, BF16) for shape in outs],
        scratch_shapes=[
            pltpu.VMEM((strip, features), BF16),
            pltpu.VMEM(w_obs.shape, BF16),
            pltpu.VMEM(w_out.shape, BF16),
            pltpu.VMEM((2, strip, channels), BF16),
            pltpu.VMEM((groups, strip, GROUP), BF16),
            pltpu.SemaphoreType.DMA((3,)),
        ],
        compiler_params=pltpu.CompilerParams(vmem_limit_bytes=32 * MIB),
        cost_estimate=pl.CostEstimate(
            flops=14 * strip * features * features,
            bytes_accessed=12 * strip * features + 8 * features * features,
            transcendentals=strip * CELLS * bias.shape[0],
        ),
    )(packed, scale, gain, base, folded, bias, ordered, w_obs, w_out, *extra)


def corner_kernel(lon_cells, block_ref, edge_ref):
    size = block_ref.shape[0]
    line, moved = divided(lax.broadcasted_iota(jnp.int32, (1, size), 1), lon_cells)
    wanted = jnp.where(moved < HALF_O, line * HALF_O + moved, -1)
    index = lax.broadcasted_iota(jnp.int32, (EDGE, 1), 0)
    edge_ref[...] = dot(selection(index, wanted), block_ref[...]).astype(BF16)


def corner(block, lon_cells):
    size, features = block.shape
    return pl.pallas_call(
        functools.partial(corner_kernel, lon_cells),
        out_shape=jax.ShapeDtypeStruct((EDGE, features), BF16),
        compiler_params=pltpu.CompilerParams(vmem_limit_bytes=16 * MIB),
        cost_estimate=pl.CostEstimate(
            flops=2 * EDGE * size * features, bytes_accessed=2 * size * features, transcendentals=0
        ),
    )(block)


def join_kernel(lon_cells, count, *refs):
    ins, out_ref = refs[:-1], refs[-1]
    size = WL * HALF_A * lon_cells
    row = lax.broadcasted_iota(jnp.int32, (size, 1), 0)
    line, moved = divided(row, lon_cells)
    edge = jnp.where(moved < HALF_O, line * HALF_O + moved, -1)
    insert = selection(edge, lax.broadcasted_iota(jnp.int32, (1, EDGE), 1))
    for at in range(count):

        @pl.when(pl.program_id(0) == at)
        def _():
            block_ref, edge_ref = ins[2 * at : 2 * at + 2]
            west = dot(insert, edge_ref[...])
            full = jnp.where(moved < HALF_O, west, block_ref[...].astype(F32)).astype(BF16)
            half = size // WL
            for l in range(WL):
                out_ref[l, 0] = full[l * half : (l + 1) * half]


def join(blocks, lon_cells):
    features = blocks[0][0].shape[-1]
    size = WL * HALF_A * lon_cells
    flat, specs = [], []
    for block, edges, at in blocks:
        flat += [block, edges]
        specs.append(pl.BlockSpec((size, features), lambda i: (0, 0)))
        specs.append(pl.BlockSpec((EDGE, features), lambda i, at=at: (at, 0)))
    return pl.pallas_call(
        functools.partial(join_kernel, lon_cells, len(blocks)),
        grid=(len(blocks),),
        in_specs=specs,
        out_specs=pl.BlockSpec((WL, 1, size // WL, features), lambda i: (0, i, 0, 0)),
        out_shape=jax.ShapeDtypeStruct((WL, len(blocks), size // WL, features), BF16),
        compiler_params=pltpu.CompilerParams(vmem_limit_bytes=16 * MIB),
        cost_estimate=pl.CostEstimate(
            flops=0, bytes_accessed=4 * len(blocks) * size * features, transcendentals=0
        ),
    )(*flat)


def body(
    latent_state,
    obs_rows,
    obs_cells,
    obs_counts,
    w_obs,
    w_qkv,
    w_out,
    logit_scale,
    pos_bias,
    out_gain,
):
    levels, lat_cells, lon_cells, features = latent_state.shape
    lat_devices = lax.axis_size("lat")
    lon_devices = lax.axis_size("lon")
    devices = lat_devices * lon_devices
    both = ("lat", "lon")
    capacity = obs_rows.shape[2] // devices
    channels = obs_rows.shape[3]

    packed = pack(
        obs_rows.reshape(devices, capacity, channels),
        obs_cells.reshape(1, devices * capacity),
        obs_counts.reshape(1, devices),
    )
    packed = lax.all_to_all(packed, both, split_axis=0, concat_axis=0, tiled=True)
    base, folded, ordered, bias = project(
        latent_state.reshape(-1, features), w_obs, w_qkv, pos_bias, lon_cells
    )
    gain = out_gain[None]

    def attend(strip_at, carried=None):
        return attend_strip(
            strip_at, packed, logit_scale, gain, base, folded, bias, ordered, w_obs, w_out,
            lat_cells, lon_cells, carried,
        )

    south = [(i, i + 1) for i in range(lat_devices - 1)]
    east = [(i, (i + 1) % lon_devices) for i in range(lon_devices)]
    low_near, low_far, low_edge = attend(1)
    first = lax.ppermute(low_far, "lat", south)
    top_near, top_far, edges = attend(0, low_edge)
    edges = lax.ppermute(edges, "lon", east)
    first_edge = lax.ppermute(corner(first, lon_cells), "lon", east)
    joined = join(
        [
            (first, first_edge, 0),
            (top_near, edges, 0),
            (top_far, edges, 1),
            (low_near, edges, 2),
        ],
        lon_cells,
    )
    return joined.reshape(levels, lat_cells, lon_cells, features)


def solution(mesh):
    in_specs = (
        P(None, "lat", "lon", None),
        P("lat", "lon", None, None),
        P("lat", "lon", None),
        P("lat", "lon", None),
        P(),
        P(),
        P(),
        P(),
        P(),
        P(),
    )
    out_specs = P(None, "lat", "lon", None)
    return jax.shard_map(body, mesh=mesh, in_specs=in_specs, out_specs=out_specs, check_vma=False)
```

profile of v0, /device:TPU:0, one launch (start us, length us, event | category | flops | bytes accessed | tf_op | source)
XLA Modules:
  0.0 84.2 jit_solution(15684044211947809669)
XLA Ops:
  0.0 1.0 %copy-done = bf16[1,1,1024,256]{3,2,1,0:T(8,128)(2,1)S(1)} copy-done((bf16[1,1,1024,256]{3,2,1,0:T(8,128)(2,1)S(1)}, bf16[1,1,1024,256]{3,2,1,0:T(8,128)(2,1)}, u32[]{:S(2)}) %copy-start) | copy-done | bytes 524312
  1.0 0.0 copy-start.1
  1.0 0.7 copy-done.1
  1.7 0.0 copy-start.2
  1.7 0.7 copy-done.2
  2.4 1.1 %shard_map.100 = bf16[32,72,128]{2,1,0:T(8,128)(2,1)} custom-call(bf16[32,32,256]{2,1,0:T(8,128)(2,1)S(1)} %bitcast.6, s32[1,1024]{1,0:T(1,128)S(1)} %bitcast.7, s32[1,32]{1,0:T(1,128)S(1)} %bitcast.8), custom_call_target="tpu_custom_call" | custom-call | tf_op jit(solution)/shard_map/pallas_call | solution.py:85
  3.5 7.3 %all-to-all-start = ((bf16[32,72,128]{2,1,0:T(8,128)(2,1)}), bf16[32,72,128]{2,1,0:T(8,128)(2,1)S(1)}, u32[]{:S(2)}, u32[]{:S(2)}) async-start(bf16[32,72,128]{2,1,0:T(8,128)(2,1)} %shard_map.100), calls=%async_computation | async-start | bytes 1179648 | tf_op jit(solution)/shard_map/all_to_all | solution.py:475
  10.8 0.0 copy-start.3
  10.8 2.8 %copy-done.3 = bf16[1024,3072]{1,0:T(8,128)(2,1)S(1)} copy-done((bf16[1024,3072]{1,0:T(8,128)(2,1)S(1)}, bf16[1024,3072]{1,0:T(8,128)(2,1)}, u32[]{:S(2)}) %copy-start.3) | copy-done | bytes 6291480
  13.6 0.0 copy-start.4
  13.6 1.7 %copy-done.4 = bf16[2,24,24,1024]{3,2,1,0:T(8,128)(2,1)S(1)} copy-done((bf16[2,24,24,1024]{3,2,1,0:T(8,128)(2,1)S(1)}, bf16[2,24,24,1024]{3,2,1,0:T(8,128)(2,1)}, u32[]{:S(2)}) %copy-start.4) | copy-done | bytes 2359320
  15.2 0.0 copy-start.5
  15.2 1.7 %copy-done.5 = f32[16,144,144]{2,1,0:T(8,128)S(1)} copy-done((f32[16,144,144]{2,1,0:T(8,128)S(1)}, f32[16,144,144]{2,1,0:T(8,128)}, u32[]{:S(2)}) %copy-start.5) | copy-done | bytes 1327128
  16.9 0.0 copy-start.7
  16.9 1.0 %copy-done.7 = bf16[256,1024]{1,0:T(8,128)(2,1)S(1)} copy-done((bf16[256,1024]{1,0:T(8,128)(2,1)S(1)}, bf16[256,1024]{1,0:T(8,128)(2,1)}, u32[]{:S(2)}) %copy-start.7) | copy-done | bytes 524312
  17.9 0.0 copy-start.6
  17.9 0.0 copy-start.8
  17.9 0.0 copy-start.9
  18.0 0.0 copy-start.10
  18.0 14.7 %shard_map.101 = (f32[4,3,1152,256]{3,2,1,0:T(8,128)}, bf16[4,3,256,256]{3,2,1,0:T(8,128)(2,1)S(1)}, bf16[1152,1024]{1,0:T(8,128)(2,1)S(1)}, f32[16,144,144]{2,1,0:T(8,128)S(1)}) custom-call(bf16[1152,1024]{1,0:T(8,128)(2,1)S(1)} %bitcast.9, bf16[256,1024]{1,0:T(8,128)(2,1)S(1)} %copy-done.7, bf16[1024,3072]{1,0:T(8,128)(2,1)S(1)} %copy-done.3, ...), custom_call_target="tpu_custom_call" | custom-call | flops 8858370048 | bytes 25165824 | tf_op jit(solution)/shard_map/pallas_call | solution.py:146
  32.6 0.0 copy-start.11
  32.6 1.4 %copy-done.11 = bf16[1152,1024]{1,0:T(8,128)(2,1)} copy-done((bf16[1152,1024]{1,0:T(8,128)(2,1)}, bf16[1152,1024]{1,0:T(8,128)(2,1)S(1)}, u32[]{:S(2)}) %copy-start.11) | copy-done | bytes 2359320
  34.0 0.0 copy-start.13
  34.0 1.4 %copy-done.13 = f32[16,144,144]{2,1,0:T(8,128)} copy-done((f32[16,144,144]{2,1,0:T(8,128)}, f32[16,144,144]{2,1,0:T(8,128)S(1)}, u32[]{:S(2)}) %copy-start.13) | copy-done | bytes 1327128
  35.4 0.0 copy-start.15
  35.4 1.2 %copy-done.15 = bf16[4,3,256,256]{3,2,1,0:T(8,128)(2,1)} copy-done((bf16[4,3,256,256]{3,2,1,0:T(8,128)(2,1)}, bf16[4,3,256,256]{3,2,1,0:T(8,128)(2,1)S(1)}, u32[]{:S(2)}) %copy-start.15) | copy-done | bytes 1572888
  36.6 0.0 all-to-all-done.packed_ref
  36.6 0.0 copy-done.6
  36.6 0.0 copy-done.8
  36.6 0.0 copy-done.9
  36.6 0.0 copy-done.10
  36.6 0.0 copy-start.12
  36.6 1.7 %copy-done.12 = bf16[1152,1024]{1,0:T(8,128)(2,1)S(1)} copy-done((bf16[1152,1024]{1,0:T(8,128)(2,1)S(1)}, bf16[1152,1024]{1,0:T(8,128)(2,1)}, u32[]{:S(2)}) %copy-start.12) | copy-done | bytes 2359320
  38.3 1.7 %copy-done.14 = f32[16,144,144]{2,1,0:T(8,128)S(1)} copy-done((f32[16,144,144]{2,1,0:T(8,128)S(1)}, f32[16,144,144]{2,1,0:T(8,128)}, u32[]{:S(2)}) %copy-start.14) | copy-done | bytes 1327128
  39.9 0.0 copy-start.16
  39.9 1.4 %copy-done.16 = bf16[4,3,256,256]{3,2,1,0:T(8,128)(2,1)S(1)} copy-done((bf16[4,3,256,256]{3,2,1,0:T(8,128)(2,1)S(1)}, bf16[4,3,256,256]{3,2,1,0:T(8,128)(2,1)}, u32[]{:S(2)}) %copy-start.16) | copy-done | bytes 1572888
  41.4 0.0 copy-start.17
  41.4 13.5 %shard_map.102 = (bf16[288,1024]{1,0:T(8,128)(2,1)S(1)}, bf16[288,1024]{1,0:T(8,128)(2,1)S(1)}, bf16[48,1024]{1,0:T(8,128)(2,1)S(1)}) custom-call(bf16[32,72,128]{2,1,0:T(8,128)(2,1)S(1)} %all-to-all-done.packed_ref, f32[16]{0:T(128)S(1)} %copy-done.10, f32[1,1024]{1,0:T(1,128)S(1)} %bitcast.10, f32[4,3,1152,256]{3,2,1,0:T(8,128)} %get-tuple-element.15.base_ref, ...), custom_call_target="tpu_custom_call" | custom-call | flops 8455716864 | bytes 15466496 | tf_op jit(solution)/shard_map/pallas_call | solution.py:356
  54.8 3.9 %collective-permute-start = (bf16[288,1024]{1,0:T(8,128)(2,1)S(1)}, bf16[288,1024]{1,0:T(8,128)(2,1)S(1)}, u32[]{:S(2)}, u32[]{:S(2)}) collective-permute-start(bf16[288,1024]{1,0:T(8,128)(2,1)S(1)} %get-tuple-element.19), channel_id=1, source_target_pairs={{0,8},{8,16},{16,24},{1,9},{9,17},{17,25},{2,10},{10,18},{18,26},{... | collective-permute-start | bytes 1769480 | tf_op jit(solution)/shard_map/ppermute | solution.py:490
  58.7 0.0 copy-done.17
  58.7 13.6 %shard_map.104 = (bf16[288,1024]{1,0:T(8,128)(2,1)S(1)}, bf16[288,1024]{1,0:T(8,128)(2,1)S(1)}, bf16[144,1024]{1,0:T(8,128)(2,1)S(1)}) custom-call(bf16[32,72,128]{2,1,0:T(8,128)(2,1)S(1)} %all-to-all-done.packed_ref, f32[16]{0:T(128)S(1)} %copy-done.10, f32[1,1024]{1,0:T(1,128)S(1)} %bitcast.11, f32[4,3,1152,256]{3,2,1,0:T(8,128)} %get-tuple-element.15.base_ref, ...), custom_call_target="tpu_custom_call" | custom-call | flops 8455716864 | bytes 15466496 | tf_op jit(solution)/shard_map/pallas_call | solution.py:356
  72.3 0.1 collective-permute-start.2
  72.4 0.0 collective-permute-done.block_ref.refs_0_
  72.4 0.2 shard_map.103
  72.7 1.6 %collective-permute-start.1 = (bf16[48,1024]{1,0:T(8,128)(2,1)S(1)}, bf16[48,1024]{1,0:T(8,128)(2,1)S(1)}, u32[]{:S(2)}, u32[]{:S(2)}) collective-permute-start(bf16[48,1024]{1,0:T(8,128)(2,1)S(1)} %shard_map.103), channel_id=1, source_target_pairs={{0,1},{1,2},{2,3},{3,4},{4,5},{5,6},{6,7},{7,0},{8,9},{9,10},{10,1... | collective-permute-start | bytes 294920 | tf_op jit(solution)/shard_map/ppermute | solution.py:493
  74.3 6.1 %collective-permute-done.2.refs_3_.refs_5_.refs_7_ = bf16[144,1024]{1,0:T(8,128)(2,1)S(1)} collective-permute-done((bf16[144,1024]{1,0:T(8,128)(2,1)S(1)}, bf16[144,1024]{1,0:T(8,128)(2,1)S(1)}, u32[]{:S(2)}, u32[]{:S(2)}) %collective-permute-start.2) | collective-permute-done | bytes 294944 | tf_op jit(solution)/shard_map/ppermute | solution.py:492
  80.3 1.1 %collective-permute-done.1.refs_1_ = bf16[48,1024]{1,0:T(8,128)(2,1)S(1)} collective-permute-done((bf16[48,1024]{1,0:T(8,128)(2,1)S(1)}, bf16[48,1024]{1,0:T(8,128)(2,1)S(1)}, u32[]{:S(2)}, u32[]{:S(2)}) %collective-permute-start.1) | collective-permute-done | bytes 98336 | tf_op jit(solution)/shard_map/ppermute | solution.py:493
  81.4 2.8 %shard_map.105 = bf16[2,4,144,1024]{3,2,1,0:T(8,128)(2,1)} custom-call(bf16[288,1024]{1,0:T(8,128)(2,1)S(1)} %collective-permute-done.block_ref.refs_0_, bf16[48,1024]{1,0:T(8,128)(2,1)S(1)} %collective-permute-done.1.refs_1_, bf16[288,1024]{1,0:T(8,128)(2,1)S(1)} %get-tuple-element.21.refs_2_, ...), custom_call_target="tpu_custom_call" | custom-call | bytes 4718592 | tf_op jit(solution)/shard_map/pallas_call | solution.py:437
  (2 shorter events, 0.0 us)
Async XLA Ops:
  0.0 1.0 %copy-start = (bf16[1,1,1024,256]{3,2,1,0:T(8,128)(2,1)S(1)}, bf16[1,1,1024,256]{3,2,1,0:T(8,128)(2,1)}, u32[]{:S(2)}) copy-start(bf16[1,1,1024,256]{3,2,1,0:T(8,128)(2,1)} %param.11) | copy-start | bytes 1572868
  1.0 0.7 copy-start.1
  1.7 0.7 copy-start.2
  3.5 33.1 %all-to-all-start = ((bf16[32,72,128]{2,1,0:T(8,128)(2,1)}), bf16[32,72,128]{2,1,0:T(8,128)(2,1)S(1)}, u32[]{:S(2)}, u32[]{:S(2)}) async-start(bf16[32,72,128]{2,1,0:T(8,128)(2,1)} %shard_map.100), calls=%async_computation | async-start | bytes 1179648 | tf_op jit(solution)/shard_map/all_to_all | solution.py:475
  10.8 2.8 %copy-start.3 = (bf16[1024,3072]{1,0:T(8,128)(2,1)S(1)}, bf16[1024,3072]{1,0:T(8,128)(2,1)}, u32[]{:S(2)}) copy-start(bf16[1024,3072]{1,0:T(8,128)(2,1)} %wv_ref.1) | copy-start | bytes 18874372
  13.6 1.7 %copy-start.4 = (bf16[2,24,24,1024]{3,2,1,0:T(8,128)(2,1)S(1)}, bf16[2,24,24,1024]{3,2,1,0:T(8,128)(2,1)}, u32[]{:S(2)}) copy-start(bf16[2,24,24,1024]{3,2,1,0:T(8,128)(2,1)} %param.10) | copy-start | bytes 7077892
  15.2 1.7 %copy-start.5 = (f32[16,144,144]{2,1,0:T(8,128)S(1)}, f32[16,144,144]{2,1,0:T(8,128)}, u32[]{:S(2)}) copy-start(f32[16,144,144]{2,1,0:T(8,128)} %bias_ref.1) | copy-start | bytes 3981316
  16.9 1.0 %copy-start.7 = (bf16[256,1024]{1,0:T(8,128)(2,1)S(1)}, bf16[256,1024]{1,0:T(8,128)(2,1)}, u32[]{:S(2)}) copy-start(bf16[256,1024]{1,0:T(8,128)(2,1)} %w_obs_hbm.3) | copy-start | bytes 1572868
  17.9 18.6 %copy-start.6 = (bf16[1024,1024]{1,0:T(8,128)(2,1)S(1)}, bf16[1024,1024]{1,0:T(8,128)(2,1)}, u32[]{:S(2)}) copy-start(bf16[1024,1024]{1,0:T(8,128)(2,1)} %w_out_hbm.3) | copy-start | bytes 6291460
  17.9 18.6 %copy-start.8 = (bf16[256,1024]{1,0:T(8,128)(2,1)S(1)}, bf16[256,1024]{1,0:T(8,128)(2,1)}, u32[]{:S(2)}) copy-start(bf16[256,1024]{1,0:T(8,128)(2,1)} %w_obs_hbm.3) | copy-start | bytes 1572868
  17.9 18.6 %copy-start.9 = (f32[1024]{0:T(1024)S(1)}, f32[1024]{0:T(1024)}, u32[]{:S(2)}) copy-start(f32[1024]{0:T(1024)} %param.19) | copy-start | bytes 12292
  18.0 18.7 %copy-start.10 = (f32[16]{0:T(128)S(1)}, f32[16]{0:T(128)}, u32[]{:S(2)}) copy-start(f32[16]{0:T(128)} %scale_ref.3) | copy-start | bytes 196
  32.6 1.4 %copy-start.11 = (bf16[1152,1024]{1,0:T(8,128)(2,1)}, bf16[1152,1024]{1,0:T(8,128)(2,1)S(1)}, u32[]{:S(2)}) copy-start(bf16[1152,1024]{1,0:T(8,128)(2,1)S(1)} %get-tuple-element.18.ordered_hbm) | copy-start | bytes 7077892
  34.0 1.4 %copy-start.13 = (f32[16,144,144]{2,1,0:T(8,128)}, f32[16,144,144]{2,1,0:T(8,128)S(1)}, u32[]{:S(2)}) copy-start(f32[16,144,144]{2,1,0:T(8,128)S(1)} %get-tuple-element.17.bias_ref) | copy-start | bytes 3981316
  35.4 1.2 %copy-start.15 = (bf16[4,3,256,256]{3,2,1,0:T(8,128)(2,1)}, bf16[4,3,256,256]{3,2,1,0:T(8,128)(2,1)S(1)}, u32[]{:S(2)}) copy-start(bf16[4,3,256,256]{3,2,1,0:T(8,128)(2,1)S(1)} %get-tuple-element.16.folded_ref) | copy-start | bytes 4718596
  36.6 1.7 %copy-start.12 = (bf16[1152,1024]{1,0:T(8,128)(2,1)S(1)}, bf16[1152,1024]{1,0:T(8,128)(2,1)}, u32[]{:S(2)}) copy-start(bf16[1152,1024]{1,0:T(8,128)(2,1)} %copy-done.11) | copy-start | bytes 7077892
  38.3 1.7 %copy-start.14 = (f32[16,144,144]{2,1,0:T(8,128)S(1)}, f32[16,144,144]{2,1,0:T(8,128)}, u32[]{:S(2)}) copy-start(f32[16,144,144]{2,1,0:T(8,128)} %copy-done.13) | copy-start | bytes 3981316
  39.9 1.4 %copy-start.16 = (bf16[4,3,256,256]{3,2,1,0:T(8,128)(2,1)S(1)}, bf16[4,3,256,256]{3,2,1,0:T(8,128)(2,1)}, u32[]{:S(2)}) copy-start(bf16[4,3,256,256]{3,2,1,0:T(8,128)(2,1)} %copy-done.15) | copy-start | bytes 4718596
  41.4 17.4 %copy-start.17 = (bf16[4,3,256,256]{3,2,1,0:T(8,128)(2,1)S(1)}, bf16[4,3,256,256]{3,2,1,0:T(8,128)(2,1)}, u32[]{:S(2)}) copy-start(bf16[4,3,256,256]{3,2,1,0:T(8,128)(2,1)} %copy-done.15) | copy-start | bytes 4718596
  54.8 17.6 %collective-permute-start = (bf16[288,1024]{1,0:T(8,128)(2,1)S(1)}, bf16[288,1024]{1,0:T(8,128)(2,1)S(1)}, u32[]{:S(2)}, u32[]{:S(2)}) collective-permute-start(bf16[288,1024]{1,0:T(8,128)(2,1)S(1)} %get-tuple-element.19), channel_id=1, source_target_pairs={{0,8},{8,16},{16,24},{1,9},{9,17},{17,25},{2,10},{10,18},{18,26},{... | collective-permute-start | bytes 1769480 | tf_op jit(solution)/shard_map/ppermute | solution.py:490
  72.3 8.0 %collective-permute-start.2 = (bf16[144,1024]{1,0:T(8,128)(2,1)S(1)}, bf16[144,1024]{1,0:T(8,128)(2,1)S(1)}, u32[]{:S(2)}, u32[]{:S(2)}) collective-permute-start(bf16[144,1024]{1,0:T(8,128)(2,1)S(1)} %get-tuple-element.22), channel_id=1, source_target_pairs={{0,1},{1,2},{2,3},{3,4},{4,5},{5,6},{6,7},{7,0},{8,9},{9,10},{10,1... | collective-permute-start | bytes 884744 | tf_op jit(solution)/shard_map/ppermute | solution.py:492
  72.7 8.7 %collective-permute-start.1 = (bf16[48,1024]{1,0:T(8,128)(2,1)S(1)}, bf16[48,1024]{1,0:T(8,128)(2,1)S(1)}, u32[]{:S(2)}, u32[]{:S(2)}) collective-permute-start(bf16[48,1024]{1,0:T(8,128)(2,1)S(1)} %shard_map.103), channel_id=1, source_target_pairs={{0,1},{1,2},{2,3},{3,4},{4,5},{5,6},{6,7},{7,0},{8,9},{9,10},{10,1... | collective-permute-start | bytes 294920 | tf_op jit(solution)/shard_map/ppermute | solution.py:493
where the time goes:
time: 84.7 us; the launch traced here: 84.2 us
  Pallas kernels  45.8 us (54%)
  local copies, waits for them, and re-layouts  18.2 us (21%)
  starting transfers between devices  12.9 us (15%)
  waiting for transfers between devices  7.14 us (8%)
    pallas_call x2, Pallas kernels, attend_strip(): pl.pallas_call(functools.partial(strip_kernel, strip_at, lon_cells, lat_c...  27.1 us
    unnamed x36, local copies, waits for them, and re-layouts  18.2 us
    pallas_call x1, Pallas kernels, project(): pl.pallas_call(functools.partial(project_kernel, lon_cells), grid=(groups...  14.7 us
    all_to_all x1, starting transfers between devices, body(): lax.all_to_all(packed, both, split_axis=0, concat_axis=0, tiled=True)  7.3 us
    ppermute x1, waiting for transfers between devices, body(): edges = lax.ppermute(edges, 'lon', east)  6.08 us
    ppermute x1, starting transfers between devices, body(): first = lax.ppermute(low_far, 'lat', south)  3.89 us
    pallas_call x1, Pallas kernels, join(): pl.pallas_call(functools.partial(join_kernel, lon_cells, len(blocks)), gr...  2.76 us
  transfers between devices with their start and end apart: 4, of which 2 were waited for; matrix products, arithmetic and copies ran while one was open for 0% of the time, Pallas kernels for 34%

commit v1 on v0

--- a/solution.py
+++ b/solution.py
@@ -49,6 +49,10 @@
 
 def selection(rows, columns):
     return (rows == columns).astype(F32).astype(BF16)
+
+
+def pinned(x):
+    return pltpu.with_memory_space_constraint(x, pltpu.HBM)
 
 
 def pack_kernel(rows_ref, cells_ref, counts_ref, packed_ref):
@@ -86,7 +90,7 @@
         pack_kernel,
         out_shape=jax.ShapeDtypeStruct((devices, held, LANES), BF16),
         compiler_params=pltpu.CompilerParams(vmem_limit_bytes=16 * MIB),
-    )(rows, cells, counts)
+    )(pinned(rows), pinned(cells), pinned(counts))
 
 
 def project_kernel(
@@ -99,7 +103,6 @@
     bias_ref,
     base_ref,
     folded_ref,
-    ordered_ref,
     scaled_ref,
     left,
 ):
@@ -122,9 +125,7 @@
                 ],
                 axis=0,
             )
-            moved = dot(perm, cells).astype(BF16)
-            left[s * strip : (s + 1) * strip] = moved
-            ordered_ref[s * strip : (s + 1) * strip] = moved
+            left[s * strip : (s + 1) * strip] = dot(perm, cells).astype(BF16)
         left[rows:] = w_obs_ref[...]
 
     for i, w_ref in enumerate((wq_ref, wk_ref, wv_ref)):
@@ -157,14 +158,12 @@
         out_specs=[
             pl.BlockSpec((1, 3, rows, GROUP), lambda i: (i, 0, 0, 0)),
             pl.BlockSpec((1, 3, channels, GROUP), lambda i: (i, 0, 0, 0)),
-            pl.BlockSpec((rows, features), whole),
             some_heads,
         ],
         out_shape=[
-            jax.ShapeDtypeStruct((groups, 3, rows, GROUP), F32),
-            jax.ShapeDtypeStruct((groups, 3, channels, GROUP), BF16),
-            jax.ShapeDtypeStruct((rows, features), BF16),
-            jax.ShapeDtypeStruct(bias.shape, F32),
+            pltpu.HBM((groups, 3, rows, GROUP), F32),
+            pltpu.HBM((groups, 3, channels, GROUP), BF16),
+            pltpu.HBM(bias.shape, F32),
         ],
         scratch_shapes=[pltpu.VMEM((rows + channels, features), BF16)],
         compiler_params=pltpu.CompilerParams(vmem_limit_bytes=32 * MIB),
@@ -173,13 +172,28 @@
             bytes_accessed=4 * rows * columns + 2 * features * columns + 4 * rows * features,
             transcendentals=0,
         ),
-    )(latent, w_obs, w_qkv, w_qkv, w_qkv, bias)
+    )(pinned(latent), pinned(w_obs), *[pinned(w_qkv)] * 3, pinned(bias))
+
+
+def in_output_order(target, at, window, block, lon_cells):
+    for level in range(WL):
+        for lat in range(WA):
+            half, line = divmod(lat, HALF_A)
+            row = (half * WL + (level + WL // 2) % WL) * HALF_A + line
+            source = (level * WA + lat) * WO
+            moved = window * WO + HALF_O
+            begin = 0
+            while begin < WO:
+                goal = (moved + begin) % lon_cells
+                count = min(WO - begin, lon_cells - goal)
+                lines = slice(row * lon_cells + goal, row * lon_cells + goal + count)
+                target[lines, at] = block[source + begin : source + begin + count]
+                begin += count
 
 
 def strip_kernel(
     strip_at,
     lon_cells,
-    lat_cells,
     passed,
     packed_ref,
     scale_ref,
@@ -187,17 +201,28 @@
     base_ref,
     folded_ref,
     bias_ref,
-    ordered_hbm,
+    latent_hbm,
     w_obs_hbm,
     w_out_hbm,
     *rest,
 ):
     carried_ref = rest[0] if passed else None
-    near_ref, far_ref, edge_ref, ordered_ref, w_obs_ref, w_out_ref, gathered, context, sems = rest[
-        passed:
-    ]
+    (
+        near_ref,
+        far_ref,
+        edge_ref,
+        latent_ref,
+        w_obs_ref,
+        w_out_ref,
+        gathered,
+        gathered_out,
+        context,
+        sems,
+    ) = rest[passed:]
     step = pl.program_id(0)
-    strip, features = ordered_ref.shape
+    lat_cells = latent_hbm.shape[1]
+    features = w_out_ref.shape[0]
+    strip = gathered.shape[0]
     windows = strip // CELLS
     groups = features // GROUP
     heads = bias_ref.shape[0]
@@ -207,7 +232,9 @@
     cuts = channels // LANES
     capacity = (held - EXTRA) // cuts
     copies = [
-        pltpu.make_async_copy(ordered_hbm.at[pl.ds(strip_at * strip, strip)], ordered_ref, sems.at[0]),
+        pltpu.make_async_copy(
+            latent_hbm.at[:, pl.ds(strip_at * WA, WA)], latent_ref, sems.at[0]
+        ),
         pltpu.make_async_copy(w_obs_hbm, w_obs_ref, sems.at[1]),
         pltpu.make_async_copy(w_out_hbm, w_out_ref, sems.at[2]),
     ]
@@ -241,9 +268,10 @@
             ]
             rows = jnp.concatenate(rows, axis=1)
             total += dot(selection(cell, target.astype(jnp.int32)), rows)
-        high = total.astype(BF16)
-        gathered[0] = high
-        gathered[1] = (total - high.astype(F32)).astype(BF16)
+        gathered[...] = total.astype(BF16)
+        for w in range(windows):
+            block = total[w * CELLS : (w + 1) * CELLS]
+            in_output_order(gathered_out, slice(None), w, block, lon_cells)
 
     lane_head = lax.broadcasted_iota(jnp.int32, (1, GROUP), 1) // width
     same_head = selection(lax.broadcasted_iota(jnp.int32, (GROUP, 1), 0) // width, lane_head)
@@ -253,23 +281,23 @@
     left_half = lax.broadcasted_iota(jnp.int32, (CELLS, 2 * width), 1) < width
     blank = jnp.zeros((width, CELLS), BF16)
 
-    high = gathered[0]
+    high = gathered[...]
     query, keys, values = (base_ref[0, i] + dot(high, folded_ref[0, i]) for i in range(3))
     query_sum = dot((query * query).astype(BF16), same_head)
-    keys_sum = dot((keys * keys).astype(BF16), same_head)
     query_n = (query * (lax.rsqrt(query_sum + cosine_eps) * scale)).astype(BF16)
-    keys_n = keys * lax.rsqrt(keys_sum + cosine_eps)
 
     def scored(w):
         here = slice(w * CELLS, (w + 1) * CELLS)
-        keys_t = keys_n[here].T.astype(BF16)
+        keys_t = keys[here].T
         result = []
         for h in range(heads):
             pair, side = h // 2, h % 2
             lanes = slice(2 * pair * width, 2 * (pair + 1) * width)
-            picked = keys_t[h * width : (h + 1) * width]
-            picked = jnp.concatenate([blank, picked] if side else [picked, blank], axis=0)
-            result.append(dot(query_n[here, lanes], picked))
+            own = keys_t[h * width : (h + 1) * width]
+            own = own * lax.rsqrt(jnp.sum(own * own, 0, keepdims=True) + cosine_eps)
+            own = own.astype(BF16)
+            own = jnp.concatenate([blank, own] if side else [own, blank], axis=0)
+            result.append(dot(query_n[here, lanes], own))
         return result
 
     def weighted(w, scores):
@@ -283,8 +311,11 @@
         parts = []
         for a, b in zip(sums[::2], sums[1::2]):
             norm = pltpu.roll(jnp.where(left_half, b, a), width, 1)
-            parts.append(jnp.where(left_half, a, b) / norm)
-        context[step, here] = jnp.concatenate(parts, axis=1).astype(BF16)
+            guess = pl.reciprocal(norm, approx=True)
+            parts.append(jnp.where(left_half, a, b) * (guess * (2.0 - norm * guess)))
+        in_output_order(
+            context.at[step], slice(None), w, jnp.concatenate(parts, axis=1), lon_cells
+        )
 
     scores = scored(0)
     for w in range(windows):
@@ -296,53 +327,45 @@
     def _():
         for copy in copies:
             copy.wait()
-        pieces = 2
-        size = strip // pieces
-        cuts = [slice(at * size, (at + 1) * size) for at in range(pieces)]
+        size = strip // 2
+        line, moved = divided(lax.broadcasted_iota(jnp.int32, (1, size), 1), lon_cells)
+        wanted = jnp.where(moved < HALF_O, line * HALF_O + moved, -1)
+        pick = selection(lax.broadcasted_iota(jnp.int32, (EDGE, 1), 0), wanted)
+        halves = [slice(h * size, (h + 1) * size) for h in range(2)]
         projs = [
-            dot(jnp.concatenate([context[g, cut] for g in range(groups)], axis=1), w_out_ref[...])
-            for cut in cuts
+            dot(
+                jnp.concatenate([context[g, here].astype(BF16) for g in range(groups)], axis=1),
+                w_out_ref[...],
+            )
+            for here in halves
         ]
-        latents = [
-            ordered_ref[cut].astype(F32)
-            + dot(gathered[0, cut], w_obs_ref[...])
-            + dot(gathered[1, cut], w_obs_ref[...])
-            for cut in cuts
-        ]
-        done = []
-        for proj, latent in zip(projs, latents):
+        added = [dot(gathered_out[here].astype(BF16), w_obs_ref[...]) for here in halves]
+        for h, out_ref in enumerate((near_ref, far_ref)):
+            runs = []
+            for l in range(WL):
+                own = latent_ref[(l - WL // 2) % WL, h * HALF_A : (h + 1) * HALF_A].astype(F32)
+                own = jnp.concatenate(
+                    [own[:, lon_cells - HALF_O :], own[:, : lon_cells - HALF_O]], axis=1
+                )
+                runs.append(own.reshape(HALF_A * lon_cells, features))
+            latent = jnp.concatenate(runs, axis=0) + added[h]
+            proj = projs[h]
             center = proj - jnp.mean(proj, -1, keepdims=True)
             spread = jnp.mean(center * center, -1, keepdims=True)
             normed = center * lax.rsqrt(spread + layer_eps) * gain_ref[...]
-            done.append((latent + normed).astype(BF16))
-        done = jnp.concatenate(done, axis=0)
-        row = lax.broadcasted_iota(jnp.int32, (1, strip), 1)
-        window, level, lat, lon = window_parts(row)
-        level = lax.rem(level + WL // 2, jnp.full_like(level, WL))
-        half, lat = divided(lat, HALF_A)
-        lon = window * WO + lon
-        moved = lax.rem(lon + HALF_O, jnp.full_like(lon, lon_cells))
-        place = ((half * WL + level) * HALF_A + lat) * lon_cells + moved
-        edge = (level * HALF_A + lat) * HALF_O + moved
-        size = WL * HALF_A * lon_cells
-        for h, out_ref in enumerate((near_ref, far_ref)):
-            index = lax.broadcasted_iota(jnp.int32, (size, 1), 0) + h * size
-            out_ref[...] = dot(selection(index, place), done).astype(BF16)
+            done = (latent + normed).astype(BF16)
+            out_ref[...] = done
             if h == 0 or passed:
-                index = lax.broadcasted_iota(jnp.int32, (EDGE, 1), 0)
-                wanted = jnp.where((moved < HALF_O) & (half == h), edge, -1)
-                chosen = dot(selection(index, wanted), done).astype(BF16)
-                edge_ref[h * EDGE : (h + 1) * EDGE] = chosen
+                edge_ref[h * EDGE : (h + 1) * EDGE] = dot(pick, done).astype(BF16)
         if passed:
             edge_ref[2 * EDGE :] = carried_ref[...]
 
 
 def attend_strip(
-    strip_at, packed, scale, gain, base, folded, bias, ordered, w_obs, w_out, lat_cells, lon_cells,
-    carried=None,
+    strip_at, packed, scale, gain, base, folded, bias, latent, w_obs, w_out, carried=None
 ):
+    levels, lat_cells, lon_cells, features = latent.shape
     strip = WL * WA * lon_cells
-    features = w_out.shape[0]
     groups = features // GROUP
     channels = w_obs.shape[0]
     heads = bias.shape[0] // groups
@@ -354,7 +377,7 @@
     outs = [half, half, (3 * EDGE if passed else EDGE, features)]
     extra = [carried] if passed else []
     return pl.pallas_call(
-        functools.partial(strip_kernel, strip_at, lon_cells, lat_cells, passed),
+        functools.partial(strip_kernel, strip_at, lon_cells, passed),
         grid=(groups,),
         in_specs=[
             pl.BlockSpec(packed.shape, lambda i: (0, 0, 0), pipeline_mode=once),
@@ -371,20 +394,32 @@
         out_specs=[pl.BlockSpec(shape, whole) for shape in outs],
         out_shape=[jax.ShapeDtypeStruct(shape, BF16) for shape in outs],
         scratch_shapes=[
-            pltpu.VMEM((strip, features), BF16),
+            pltpu.VMEM((levels, WA, lon_cells, features), BF16),
             pltpu.VMEM(w_obs.shape, BF16),
             pltpu.VMEM(w_out.shape, BF16),
-            pltpu.VMEM((2, strip, channels), BF16),
-            pltpu.VMEM((groups, strip, GROUP), BF16),
+            pltpu.VMEM((strip, channels), BF16),
+            pltpu.VMEM((strip, channels), F32),
+            pltpu.VMEM((groups, strip, GROUP), F32),
             pltpu.SemaphoreType.DMA((3,)),
         ],
-        compiler_params=pltpu.CompilerParams(vmem_limit_bytes=32 * MIB),
+        compiler_params=pltpu.CompilerParams(vmem_limit_bytes=40 * MIB),
         cost_estimate=pl.CostEstimate(
             flops=14 * strip * features * features,
             bytes_accessed=12 * strip * features + 8 * features * features,
             transcendentals=strip * CELLS * bias.shape[0],
         ),
-    )(packed, scale, gain, base, folded, bias, ordered, w_obs, w_out, *extra)
+    )(
+        packed,
+        scale,
+        pinned(gain),
+        pinned(base),
+        pinned(folded),
+        pinned(bias),
+        pinned(latent),
+        pinned(w_obs),
+        pinned(w_out),
+        *extra,
+    )
 
 
 def corner_kernel(lon_cells, block_ref, edge_ref):
@@ -473,15 +508,14 @@
         obs_counts.reshape(1, devices),
     )
     packed = lax.all_to_all(packed, both, split_axis=0, concat_axis=0, tiled=True)
-    base, folded, ordered, bias = project(
+    base, folded, bias = project(
         latent_state.reshape(-1, features), w_obs, w_qkv, pos_bias, lon_cells
     )
     gain = out_gain[None]
 
     def attend(strip_at, carried=None):
         return attend_strip(
-            strip_at, packed, logit_scale, gain, base, folded, bias, ordered, w_obs, w_out,
-            lat_cells, lon_cells, carried,
+            strip_at, packed, logit_scale, gain, base, folded, bias, latent_state, w_obs, w_out, carried
         )
 
     south = [(i, i + 1) for i in range(lat_devices - 1)]

time: 84.7 us -> 66.7 us (0.79)
  local copies, waits for them, and re-layouts: 18.2 us -> 0.01 us
  waiting for transfers between devices: 7.14 us -> 8.15 us
  starting transfers between devices: 12.9 us -> 11.9 us
    unnamed x36 -> x2, local copies, waits for them, and re-layouts: 18.2 us -> 0.01 us
    pallas_call x2, Pallas kernels: 27.1 us -> 23.6 us  [attend_strip(): pl.pallas_call(functools.partial(strip_kernel, strip_at, lon_cells, passe...]
    pallas_call x1, Pallas kernels: 14.7 us -> 17.4 us  [project(): pl.pallas_call(functools.partial(project_kernel, lon_cells), grid=(groups...]
    pallas_call x1, Pallas kernels: 1.09 us -> 2.2 us  [pack(): pl.pallas_call(pack_kernel, out_shape=jax.ShapeDtypeStruct((devices, held...]
  transfers between devices with their start and end apart: 4 -> 4, of which waited for: 2 -> 4; matrix products, arithmetic and copies ran while one was open for 0% -> 0% of each run, Pallas kernels for 34% -> 45%
where the time goes in v1:
time: 66.7 us; the launch traced here: 66.3 us
  Pallas kernels  46.2 us (69%)
  starting transfers between devices  11.9 us (18%)
  waiting for transfers between devices  8.15 us (12%)
    pallas_call x2, Pallas kernels, attend_strip(): pl.pallas_call(functools.partial(strip_kernel, strip_at, lon_cells, passe...  23.6 us
    pallas_call x1, Pallas kernels, project(): pl.pallas_call(functools.partial(project_kernel, lon_cells), grid=(groups...  17.4 us
    all_to_all x1, starting transfers between devices, body(): lax.all_to_all(packed, both, split_axis=0, concat_axis=0, tiled=True)  7.3 us
    ppermute x1, waiting for transfers between devices, body(): edges = lax.ppermute(edges, 'lon', east)  6.08 us
    ppermute x1, starting transfers between devices, body(): first = lax.ppermute(low_far, 'lat', south)  3.55 us
    pallas_call x1, Pallas kernels, join(): pl.pallas_call(functools.partial(join_kernel, lon_cells, len(blocks)), gr...  2.76 us
    pallas_call x1, Pallas kernels, pack(): pl.pallas_call(pack_kernel, out_shape=jax.ShapeDtypeStruct((devices, held...  2.2 us
  transfers between devices with their start and end apart: 4, of which 4 were waited for; matrix products, arithmetic and copies ran while one was open for 0% of the time, Pallas kernels for 45%

profile of v1, /device:TPU:0, one launch (start us, length us, event | category | flops | bytes accessed | tf_op | source)
XLA Modules:
  0.0 66.3 jit_solution(18349254164712993286)
XLA Ops:
  0.0 2.2 %shard_map.100 = bf16[32,72,128]{2,1,0:T(8,128)(2,1)} custom-call(bf16[32,32,256]{2,1,0:T(8,128)(2,1)} %bitcast.6, s32[1,1024]{1,0:T(1,128)} %bitcast.7, s32[1,32]{1,0:T(1,128)} %bitcast.8), custom_call_target="tpu_custom_call" | custom-call | tf_op jit(solution)/shard_map/pallas_call | solution.py:89
  2.2 7.3 %all-to-all-start = ((bf16[32,72,128]{2,1,0:T(8,128)(2,1)}), bf16[32,72,128]{2,1,0:T(8,128)(2,1)S(1)}, u32[]{:S(2)}, u32[]{:S(2)}) async-start(bf16[32,72,128]{2,1,0:T(8,128)(2,1)} %shard_map.100), calls=%async_computation | async-start | bytes 1179648 | tf_op jit(solution)/shard_map/all_to_all | solution.py:510
  9.5 0.0 copy-start
  9.5 17.4 %shard_map.101 = (f32[4,3,1152,256]{3,2,1,0:T(8,128)}, bf16[4,3,256,256]{3,2,1,0:T(8,128)(2,1)}, f32[16,144,144]{2,1,0:T(8,128)}) custom-call(bf16[1152,1024]{1,0:T(8,128)(2,1)} %bitcast.9, bf16[256,1024]{1,0:T(8,128)(2,1)} %w_obs_hbm.3, bf16[1024,3072]{1,0:T(8,128)(2,1)} %wv_ref.1, bf16[1024,3072]{1,0:T(8,128)(2,1)} %wv_ref.1, bf16[1024,3072]{1,0:T(8,128)(2,1)} %wv_ref.1, ...), custom_call_target="tpu_custom_call" | custom-call | flops 8858370048 | bytes 25165824 | tf_op jit(solution)/shard_map/pallas_call | solution.py:147
  26.9 0.4 all-to-all-done.packed_ref
  27.3 0.0 copy-done
  27.3 11.7 %shard_map.102 = (bf16[288,1024]{1,0:T(8,128)(2,1)S(1)}, bf16[288,1024]{1,0:T(8,128)(2,1)S(1)}, bf16[48,1024]{1,0:T(8,128)(2,1)S(1)}) custom-call(bf16[32,72,128]{2,1,0:T(8,128)(2,1)S(1)} %all-to-all-done.packed_ref, f32[16]{0:T(128)S(1)} %copy-done, f32[1,1024]{1,0:T(1,128)} %bitcast.10, f32[4,3,1152,256]{3,2,1,0:T(8,128)} %get-tuple-element.14.base_ref, ...), custom_call_target="tpu_custom_call" | custom-call | flops 8455716864 | bytes 15466496 | tf_op jit(solution)/shard_map/pallas_call | solution.py:379
  39.0 3.6 %collective-permute-start = (bf16[288,1024]{1,0:T(8,128)(2,1)S(1)}, bf16[288,1024]{1,0:T(8,128)(2,1)S(1)}, u32[]{:S(2)}, u32[]{:S(2)}) collective-permute-start(bf16[288,1024]{1,0:T(8,128)(2,1)S(1)} %get-tuple-element.17), channel_id=1, source_target_pairs={{0,8},{8,16},{16,24},{1,9},{9,17},{17,25},{2,10},{10,18},{18,26},{... | collective-permute-start | bytes 1769480 | tf_op jit(solution)/shard_map/ppermute | solution.py:524
  42.5 11.9 %shard_map.104 = (bf16[288,1024]{1,0:T(8,128)(2,1)S(1)}, bf16[288,1024]{1,0:T(8,128)(2,1)S(1)}, bf16[144,1024]{1,0:T(8,128)(2,1)S(1)}) custom-call(bf16[32,72,128]{2,1,0:T(8,128)(2,1)S(1)} %all-to-all-done.packed_ref, f32[16]{0:T(128)S(1)} %copy-done, f32[1,1024]{1,0:T(1,128)} %bitcast.11, f32[4,3,1152,256]{3,2,1,0:T(8,128)} %get-tuple-element.14.base_ref, ...), custom_call_target="tpu_custom_call" | custom-call | flops 8455716864 | bytes 15466496 | tf_op jit(solution)/shard_map/pallas_call | solution.py:379
  54.5 0.1 collective-permute-start.2
  54.5 0.7 %collective-permute-done.block_ref.refs_0_ = bf16[288,1024]{1,0:T(8,128)(2,1)S(1)} collective-permute-done((bf16[288,1024]{1,0:T(8,128)(2,1)S(1)}, bf16[288,1024]{1,0:T(8,128)(2,1)S(1)}, u32[]{:S(2)}, u32[]{:S(2)}) %collective-permute-start) | collective-permute-done | bytes 589856 | tf_op jit(solution)/shard_map/ppermute | solution.py:524
  55.2 0.2 shard_map.103
  55.4 1.0 %collective-permute-start.1 = (bf16[48,1024]{1,0:T(8,128)(2,1)S(1)}, bf16[48,1024]{1,0:T(8,128)(2,1)S(1)}, u32[]{:S(2)}, u32[]{:S(2)}) collective-permute-start(bf16[48,1024]{1,0:T(8,128)(2,1)S(1)} %shard_map.103), channel_id=1, source_target_pairs={{0,1},{1,2},{2,3},{3,4},{4,5},{5,6},{6,7},{7,0},{8,9},{9,10},{10,1... | collective-permute-start | bytes 294920 | tf_op jit(solution)/shard_map/ppermute | solution.py:527
  56.4 6.1 %collective-permute-done.2.refs_3_.refs_5_.refs_7_ = bf16[144,1024]{1,0:T(8,128)(2,1)S(1)} collective-permute-done((bf16[144,1024]{1,0:T(8,128)(2,1)S(1)}, bf16[144,1024]{1,0:T(8,128)(2,1)S(1)}, u32[]{:S(2)}, u32[]{:S(2)}) %collective-permute-start.2) | collective-permute-done | bytes 294944 | tf_op jit(solution)/shard_map/ppermute | solution.py:526
  62.5 1.1 %collective-permute-done.1.refs_1_ = bf16[48,1024]{1,0:T(8,128)(2,1)S(1)} collective-permute-done((bf16[48,1024]{1,0:T(8,128)(2,1)S(1)}, bf16[48,1024]{1,0:T(8,128)(2,1)S(1)}, u32[]{:S(2)}, u32[]{:S(2)}) %collective-permute-start.1) | collective-permute-done | bytes 98336 | tf_op jit(solution)/shard_map/ppermute | solution.py:527
  63.5 2.8 %shard_map.105 = bf16[2,4,144,1024]{3,2,1,0:T(8,128)(2,1)} custom-call(bf16[288,1024]{1,0:T(8,128)(2,1)S(1)} %collective-permute-done.block_ref.refs_0_, bf16[48,1024]{1,0:T(8,128)(2,1)S(1)} %collective-permute-done.1.refs_1_, bf16[288,1024]{1,0:T(8,128)(2,1)S(1)} %get-tuple-element.19.refs_2_, ...), custom_call_target="tpu_custom_call" | custom-call | bytes 4718592 | tf_op jit(solution)/shard_map/pallas_call | solution.py:472
Async XLA Ops:
  2.2 25.1 %all-to-all-start = ((bf16[32,72,128]{2,1,0:T(8,128)(2,1)}), bf16[32,72,128]{2,1,0:T(8,128)(2,1)S(1)}, u32[]{:S(2)}, u32[]{:S(2)}) async-start(bf16[32,72,128]{2,1,0:T(8,128)(2,1)} %shard_map.100), calls=%async_computation | async-start | bytes 1179648 | tf_op jit(solution)/shard_map/all_to_all | solution.py:510
  9.5 17.8 %copy-start = (f32[16]{0:T(128)S(1)}, f32[16]{0:T(128)}, u32[]{:S(2)}) copy-start(f32[16]{0:T(128)} %scale_ref.3) | copy-start | bytes 196
  39.0 16.2 %collective-permute-start = (bf16[288,1024]{1,0:T(8,128)(2,1)S(1)}, bf16[288,1024]{1,0:T(8,128)(2,1)S(1)}, u32[]{:S(2)}, u32[]{:S(2)}) collective-permute-start(bf16[288,1024]{1,0:T(8,128)(2,1)S(1)} %get-tuple-element.17), channel_id=1, source_target_pairs={{0,8},{8,16},{16,24},{1,9},{9,17},{17,25},{2,10},{10,18},{18,26},{... | collective-permute-start | bytes 1769480 | tf_op jit(solution)/shard_map/ppermute | solution.py:524
  54.5 8.0 %collective-permute-start.2 = (bf16[144,1024]{1,0:T(8,128)(2,1)S(1)}, bf16[144,1024]{1,0:T(8,128)(2,1)S(1)}, u32[]{:S(2)}, u32[]{:S(2)}) collective-permute-start(bf16[144,1024]{1,0:T(8,128)(2,1)S(1)} %get-tuple-element.20), channel_id=1, source_target_pairs={{0,1},{1,2},{2,3},{3,4},{4,5},{5,6},{6,7},{7,0},{8,9},{9,10},{10,1... | collective-permute-start | bytes 884744 | tf_op jit(solution)/shard_map/ppermute | solution.py:526
  55.4 8.1 %collective-permute-start.1 = (bf16[48,1024]{1,0:T(8,128)(2,1)S(1)}, bf16[48,1024]{1,0:T(8,128)(2,1)S(1)}, u32[]{:S(2)}, u32[]{:S(2)}) collective-permute-start(bf16[48,1024]{1,0:T(8,128)(2,1)S(1)} %shard_map.103), channel_id=1, source_target_pairs={{0,1},{1,2},{2,3},{3,4},{4,5},{5,6},{6,7},{7,0},{8,9},{9,10},{10,1... | collective-permute-start | bytes 294920 | tf_op jit(solution)/shard_map/ppermute | solution.py:527

commit v2 on v1

v2 whole, which is shorter than its diff:
```python
import functools
import math

import jax
import jax.numpy as jnp
from jax import lax
from jax.experimental import pallas as pl
from jax.experimental.pallas import tpu as pltpu
from jax.sharding import PartitionSpec as P

WL = 2
WA = 12
WO = 6
CELLS = WL * WA * WO
HALF_A = WA // 2
HALF_O = WO // 2
GROUP = 256
EXTRA = 8
BLOCK = 32
DIGIT = 32
DEAD = 255
EDGE = 48

cosine_eps = 1e-06
layer_eps = 1e-05
LOG2E = math.log2(math.e)
MIB = 1024 * 1024
LANES = 128

F32 = jnp.float32
BF16 = jnp.bfloat16


def divided(x, n):
    quotient = lax.div(x, jnp.full_like(x, n))
    return quotient, x - quotient * n


def window_parts(row):
    window, inner = divided(row, CELLS)
    level, inner = divided(inner, WA * WO)
    lat, lon = divided(inner, WO)
    return window, level, lat, lon


def dot(a, b):
    return jnp.dot(a, b, preferred_element_type=F32)


def selection(rows, columns):
    return (rows == columns).astype(F32).astype(BF16)


def pinned(x):
    return pltpu.with_memory_space_constraint(x, pltpu.HBM)


def pack_kernel(rows_ref, cells_ref, counts_ref, packed_ref):
    devices, capacity, channels = rows_ref.shape
    slots = devices * capacity
    for at in range(channels // LANES):
        part = rows_ref[:, :, at * LANES : (at + 1) * LANES]
        packed_ref[:, at * capacity : (at + 1) * capacity] = part
    cells = cells_ref[...]
    high = lax.div(cells, jnp.full_like(cells, DIGIT))
    low = cells - high * DIGIT
    slot = lax.broadcasted_iota(jnp.int32, (1, slots), 1)
    device = lax.broadcasted_iota(jnp.int32, (devices, 1), 0)
    place = lax.broadcasted_iota(jnp.int32, (slots, 1), 0)
    place = lax.rem(place, jnp.full_like(place, capacity))
    lane = lax.broadcasted_iota(jnp.int32, (1, LANES), 1)
    own = divided(slot, capacity)[0] == device
    digits = jnp.zeros((devices, LANES), F32)
    for i, digit in enumerate((high, low)):
        spread = jnp.where(own, digit.astype(F32), 0.0).astype(BF16)
        digits += dot(spread, selection(place + i * capacity, lane))
    same = device == lax.broadcasted_iota(jnp.int32, (1, devices), 1)
    count = jnp.sum(jnp.where(same, counts_ref[...].astype(F32), 0.0), -1, keepdims=True)
    dead = (lane < capacity) & (lane.astype(F32) >= count)
    digits = jnp.where(dead, float(DEAD), digits)
    packed_ref[:, channels // LANES * capacity :] = jnp.broadcast_to(
        digits[:, None, :], (devices, EXTRA, LANES)
    ).astype(BF16)


def pack(rows, cells, counts):
    devices, capacity, channels = rows.shape
    held = channels // LANES * capacity + EXTRA
    return pl.pallas_call(
        pack_kernel,
        out_shape=jax.ShapeDtypeStruct((devices, held, LANES), BF16),
        compiler_params=pltpu.CompilerParams(vmem_limit_bytes=16 * MIB),
    )(pinned(rows), pinned(cells), pinned(counts))


def project_kernel(
    lon_cells, latent_hbm, w_obs_hbm, w_hbm, bias_hbm, base_ref, folded_ref, scaled_ref, latent_ref,
    w_ref, left, sems,
):
    rows, features = latent_ref.shape
    part = WA * lon_cells
    strip = WL * part
    strips = rows // strip
    groups = features // GROUP
    windows = lon_cells // WO
    first, second = 8 * lon_cells, (WA - 8) * lon_cells

    def columns(j):
        at = lax.rem(j, 3) * groups + lax.div(j, 3)
        return pl.ds(pl.multiple_of(at * GROUP, GROUP), GROUP)

    def fetched(j):
        return pltpu.make_async_copy(w_hbm.at[:, columns(j)], w_ref.at[j], sems.at[j])

    copies = []
    for s in range(strips):
        for l in range(WL):
            lines = pl.ds((l * strips + s) * part, part)
            at = 3 * groups + len(copies)
            copies.append(
                pltpu.make_async_copy(latent_hbm.at[lines], latent_ref.at[lines], sems.at[at])
            )
    at = 3 * groups + len(copies)
    copies.append(pltpu.make_async_copy(w_obs_hbm, left.at[pl.ds(rows, w_obs_hbm.shape[0])], sems.at[at]))
    copies.append(pltpu.make_async_copy(bias_hbm, scaled_ref, sems.at[at + 1]))
    for copy in copies[:-1]:
        copy.start()
    for j in range(3 * groups):
        fetched(j).start()
    copies[-1].start()

    perms = []
    for lines in (first, second):
        run = lines // windows
        row = lax.broadcasted_iota(jnp.int32, (lines, 1), 0)
        window, inner = divided(row, run)
        lat, lon = divided(inner, WO)
        source = lat * lon_cells + window * WO + lon
        perms.append(selection(source, lax.broadcasted_iota(jnp.int32, (1, lines), 1)))
    for s in range(strips):
        moved = []
        for l in range(WL):
            copies[s * WL + l].wait()
            begin = (l * strips + s) * part
            moved.append(dot(perms[0], latent_ref[begin : begin + first]))
            moved.append(dot(perms[1], latent_ref[begin + first : begin + part]))
        for w in range(windows):
            runs = []
            for piece in moved:
                run = piece.shape[0] // windows
                runs.append(piece[w * run : (w + 1) * run])
            at = s * strip + w * CELLS
            left[at : at + CELLS] = jnp.concatenate(runs, axis=0).astype(BF16)
    copies[-2].wait()

    def multiply(j, carry):
        fetched(j).wait()
        result = dot(left[...], w_ref[j])
        base_ref[j] = result[:rows]
        folded_ref[j] = result[rows:].astype(BF16)
        return carry

    lax.fori_loop(0, 3 * groups, multiply, 0)
    copies[-1].wait()
    scaled_ref[...] = scaled_ref[...] * LOG2E


def project(latent, w_obs, w_qkv, bias, lon_cells):
    rows, features = latent.shape
    channels = w_obs.shape[0]
    columns = w_qkv.shape[1]
    blocks = columns // GROUP
    strips = rows // (WL * WA * lon_cells)
    there = pl.BlockSpec(memory_space=pl.ANY)
    here = pl.BlockSpec(memory_space=pltpu.VMEM)
    return pl.pallas_call(
        functools.partial(project_kernel, lon_cells),
        in_specs=[there] * 4,
        out_specs=[here] * 3,
        out_shape=[
            pltpu.VMEM((blocks, rows, GROUP), F32),
            pltpu.VMEM((blocks, channels, GROUP), BF16),
            pltpu.VMEM(bias.shape, F32),
        ],
        scratch_shapes=[
            pltpu.VMEM((rows, features), BF16),
            pltpu.VMEM((blocks, features, GROUP), BF16),
            pltpu.VMEM((rows + channels, features), BF16),
            pltpu.SemaphoreType.DMA((blocks + WL * strips + 2,)),
        ],
        compiler_params=pltpu.CompilerParams(vmem_limit_bytes=24 * MIB),
        cost_estimate=pl.CostEstimate(
            flops=2 * (rows + channels) * features * columns,
            bytes_accessed=4 * rows * columns + 2 * features * columns + 4 * rows * features,
            transcendentals=0,
        ),
    )(pinned(latent), pinned(w_obs), pinned(w_qkv), pinned(bias))


def in_output_order(target, at, window, block, lon_cells):
    for level in range(WL):
        for lat in range(WA):
            half, line = divmod(lat, HALF_A)
            row = (half * WL + (level + WL // 2) % WL) * HALF_A + line
            source = (level * WA + lat) * WO
            moved = window * WO + HALF_O
            begin = 0
            while begin < WO:
                goal = (moved + begin) % lon_cells
                count = min(WO - begin, lon_cells - goal)
                lines = slice(row * lon_cells + goal, row * lon_cells + goal + count)
                target[lines, at] = block[source + begin : source + begin + count]
                begin += count


def strip_kernel(
    strip_at,
    lon_cells,
    passed,
    packed_ref,
    scale_ref,
    gain_ref,
    base_ref,
    folded_ref,
    bias_ref,
    latent_hbm,
    w_obs_hbm,
    w_out_hbm,
    *rest,
):
    carried_ref = rest[0] if passed else None
    (
        near_ref,
        far_ref,
        edge_ref,
        latent_ref,
        w_obs_ref,
        w_out_ref,
        gathered,
        gathered_out,
        context,
        sems,
    ) = rest[passed:]
    lat_cells = latent_hbm.shape[1]
    features = w_out_ref.shape[0]
    strip = gathered.shape[0]
    windows = strip // CELLS
    groups = features // GROUP
    heads = bias_ref.shape[0] // groups
    width = GROUP // heads
    devices, held, _ = packed_ref.shape
    channels = w_obs_ref.shape[0]
    cuts = channels // LANES
    capacity = (held - EXTRA) // cuts
    copies = [
        pltpu.make_async_copy(
            latent_hbm.at[:, pl.ds(strip_at * WA, WA)], latent_ref, sems.at[0]
        ),
        pltpu.make_async_copy(w_obs_hbm, w_obs_ref, sems.at[1]),
        pltpu.make_async_copy(w_out_hbm, w_out_ref, sems.at[2]),
    ]

    for copy in copies:
        copy.start()
    row = lax.broadcasted_iota(jnp.int32, (strip, 1), 0)
    window, level, lat, lon = window_parts(row)
    cell = (level * lat_cells + strip_at * WA + lat) * lon_cells + window * WO + lon
    count = BLOCK * capacity
    slot = lax.broadcasted_iota(jnp.int32, (1, count), 1)
    source, place = divided(slot, capacity)
    lane = lax.broadcasted_iota(jnp.int32, (LANES, 1), 0)
    weigh = jnp.where(lane == place, float(DIGIT), 0.0) + jnp.where(
        lane == place + capacity, 1.0, 0.0
    )
    line = lax.broadcasted_iota(jnp.int32, (BLOCK * EXTRA, 1), 0)
    total = jnp.zeros((strip, channels), F32)
    for at in range(0, devices, BLOCK):
        some = slice(at, at + BLOCK)
        digits = packed_ref[some, cuts * capacity :].reshape(BLOCK * EXTRA, LANES)
        values = dot(digits, weigh.astype(BF16))
        target = jnp.sum(
            jnp.where(line == source * EXTRA, values, 0.0), 0, keepdims=True
        )
        rows = [
            packed_ref[some, c * capacity : (c + 1) * capacity].reshape(count, LANES)
            for c in range(cuts)
        ]
        rows = jnp.concatenate(rows, axis=1)
        total += dot(selection(cell, target.astype(jnp.int32)), rows)
    gathered[...] = total.astype(BF16)
    for w in range(windows):
        block = total[w * CELLS : (w + 1) * CELLS]
        in_output_order(gathered_out, slice(None), w, block, lon_cells)

    lane_head = lax.broadcasted_iota(jnp.int32, (1, GROUP), 1) // width
    same_head = selection(lax.broadcasted_iota(jnp.int32, (GROUP, 1), 0) // width, lane_head)
    left_half = lax.broadcasted_iota(jnp.int32, (CELLS, 2 * width), 1) < width
    blank = jnp.zeros((width, CELLS), BF16)

    mine = slice(strip_at * strip, (strip_at + 1) * strip)

    def group(step, carry):
        scale = jnp.zeros((1, GROUP), F32)
        for h in range(heads):
            scale = jnp.where(lane_head == h, scale_ref[step * heads + h] * LOG2E, scale)
        high = gathered[...]
        query, keys, values = (
                base_ref[3 * step + i, mine] + dot(high, folded_ref[3 * step + i]) for i in range(3)
            )
        query_sum = dot((query * query).astype(BF16), same_head)
        query_n = (query * (lax.rsqrt(query_sum + cosine_eps) * scale)).astype(BF16)

        def scored(w):
            here = slice(w * CELLS, (w + 1) * CELLS)
            keys_t = keys[here].T
            result = []
            for h in range(heads):
                pair, side = h // 2, h % 2
                lanes = slice(2 * pair * width, 2 * (pair + 1) * width)
                own = keys_t[h * width : (h + 1) * width]
                own = own * lax.rsqrt(jnp.sum(own * own, 0, keepdims=True) + cosine_eps)
                own = own.astype(BF16)
                own = jnp.concatenate([blank, own] if side else [own, blank], axis=0)
                result.append(dot(query_n[here, lanes], own))
            return result

        def weighted(w, scores):
            here = slice(w * CELLS, (w + 1) * CELLS)
            expo = [jnp.exp2(scores[h] + bias_ref[step * heads + h]).astype(BF16) for h in range(heads)]
            sums = []
            for h in range(heads):
                lanes = slice(h // 2 * 2 * width, (h // 2 + 1) * 2 * width)
                mixed = jnp.where(left_half == (h % 2 == 0), values[here, lanes], 1.0).astype(BF16)
                sums.append(dot(expo[h], mixed))
            parts = []
            for a, b in zip(sums[::2], sums[1::2]):
                norm = pltpu.roll(jnp.where(left_half, b, a), width, 1)
                guess = pl.reciprocal(norm, approx=True)
                parts.append(jnp.where(left_half, a, b) * (guess * (2.0 - norm * guess)))
            in_output_order(
                context.at[step], slice(None), w, jnp.concatenate(parts, axis=1), lon_cells
            )

        scores = scored(0)
        for w in range(windows):
            after = scored(w + 1) if w + 1 < windows else None
            weighted(w, scores)
            scores = after
        return carry

    lax.fori_loop(0, groups, group, 0)

    for copy in copies:
        copy.wait()
    size = strip // 2
    line, moved = divided(lax.broadcasted_iota(jnp.int32, (1, size), 1), lon_cells)
    wanted = jnp.where(moved < HALF_O, line * HALF_O + moved, -1)
    pick = selection(lax.broadcasted_iota(jnp.int32, (EDGE, 1), 0), wanted)
    halves = [slice(h * size, (h + 1) * size) for h in range(2)]
    projs = [
        dot(
            jnp.concatenate([context[g, here].astype(BF16) for g in range(groups)], axis=1),
            w_out_ref[...],
        )
        for here in halves
    ]
    added = [dot(gathered_out[here].astype(BF16), w_obs_ref[...]) for here in halves]
    for h, out_ref in enumerate((near_ref, far_ref)):
        runs = []
        for l in range(WL):
            own = latent_ref[(l - WL // 2) % WL, h * HALF_A : (h + 1) * HALF_A].astype(F32)
            own = jnp.concatenate(
                [own[:, lon_cells - HALF_O :], own[:, : lon_cells - HALF_O]], axis=1
            )
            runs.append(own.reshape(HALF_A * lon_cells, features))
        latent = jnp.concatenate(runs, axis=0) + added[h]
        proj = projs[h]
        center = proj - jnp.mean(proj, -1, keepdims=True)
        spread = jnp.mean(center * center, -1, keepdims=True)
        normed = center * lax.rsqrt(spread + layer_eps) * gain_ref[...]
        done = (latent + normed).astype(BF16)
        out_ref[...] = done
        if h == 0 or passed:
            edge_ref[h * EDGE : (h + 1) * EDGE] = dot(pick, done).astype(BF16)
    if passed:
        edge_ref[2 * EDGE :] = carried_ref[...]


def attend_strip(
    strip_at, packed, scale, gain, base, folded, bias, latent, w_obs, w_out, carried=None
):
    levels, lat_cells, lon_cells, features = latent.shape
    strip = WL * WA * lon_cells
    groups = features // GROUP
    channels = w_obs.shape[0]
    heads = bias.shape[0] // groups
    passed = carried is not None
    there = pl.BlockSpec(memory_space=pl.ANY)
    here = pl.BlockSpec(memory_space=pltpu.VMEM)
    half = (strip // 2, features)
    outs = [half, half, (3 * EDGE if passed else EDGE, features)]
    extra = [carried] if passed else []
    return pl.pallas_call(
        functools.partial(strip_kernel, strip_at, lon_cells, passed),
        in_specs=[here, pl.BlockSpec(memory_space=pltpu.SMEM)]
        + [here] * 4
        + [there] * 3
        + [here] * len(extra),
        out_specs=[here] * 3,
        out_shape=[jax.ShapeDtypeStruct(shape, BF16) for shape in outs],
        scratch_shapes=[
            pltpu.VMEM((levels, WA, lon_cells, features), BF16),
            pltpu.VMEM(w_obs.shape, BF16),
            pltpu.VMEM(w_out.shape, BF16),
            pltpu.VMEM((strip, channels), BF16),
            pltpu.VMEM((strip, channels), F32),
            pltpu.VMEM((groups, strip, GROUP), F32),
            pltpu.SemaphoreType.DMA((3,)),
        ],
        compiler_params=pltpu.CompilerParams(vmem_limit_bytes=24 * MIB),
        cost_estimate=pl.CostEstimate(
            flops=14 * strip * features * features,
            bytes_accessed=12 * strip * features + 8 * features * features,
            transcendentals=strip * CELLS * bias.shape[0],
        ),
    )(
        packed,
        scale,
        gain,
        base,
        folded,
        bias,
        pinned(latent),
        pinned(w_obs),
        pinned(w_out),
        *extra,
    )


def corner_kernel(lon_cells, block_ref, edge_ref):
    size = block_ref.shape[0]
    line, moved = divided(lax.broadcasted_iota(jnp.int32, (1, size), 1), lon_cells)
    wanted = jnp.where(moved < HALF_O, line * HALF_O + moved, -1)
    index = lax.broadcasted_iota(jnp.int32, (EDGE, 1), 0)
    edge_ref[...] = dot(selection(index, wanted), block_ref[...]).astype(BF16)


def corner(block, lon_cells):
    size, features = block.shape
    return pl.pallas_call(
        functools.partial(corner_kernel, lon_cells),
        out_shape=jax.ShapeDtypeStruct((EDGE, features), BF16),
        compiler_params=pltpu.CompilerParams(vmem_limit_bytes=16 * MIB),
        cost_estimate=pl.CostEstimate(
            flops=2 * EDGE * size * features, bytes_accessed=2 * size * features, transcendentals=0
        ),
    )(block)


def join_kernel(lon_cells, count, *refs):
    ins, (out_hbm, blocks, sems) = refs[:-3], refs[-3:]
    size = WL * HALF_A * lon_cells
    half = size // WL
    row = lax.broadcasted_iota(jnp.int32, (size, 1), 0)
    line, moved = divided(row, lon_cells)
    edge = jnp.where(moved < HALF_O, line * HALF_O + moved, -1)
    insert = selection(edge, lax.broadcasted_iota(jnp.int32, (1, EDGE), 1))
    copies = []
    for at in range(count):
        block_ref, edge_ref, edge_at = ins[2 * at], ins[2 * at + 1], (0, 0, 1, 2)[at]
        west = dot(insert, edge_ref[edge_at * EDGE : (edge_at + 1) * EDGE])
        full = jnp.where(moved < HALF_O, west, block_ref[...].astype(F32)).astype(BF16)
        for l in range(WL):
            blocks[at, l] = full[l * half : (l + 1) * half]
        copies.append(pltpu.make_async_copy(blocks.at[at], out_hbm.at[:, at], sems.at[at]))
        copies[-1].start()
    for copy in copies:
        copy.wait()


def join(blocks, lon_cells):
    features = blocks[0][0].shape[-1]
    size = WL * HALF_A * lon_cells
    flat = [part for block in blocks for part in block]
    return pl.pallas_call(
        functools.partial(join_kernel, lon_cells, len(blocks)),
        in_specs=[pl.BlockSpec(memory_space=pltpu.VMEM)] * len(flat),
        out_specs=pl.BlockSpec(memory_space=pl.ANY),
        out_shape=jax.ShapeDtypeStruct((WL, len(blocks), size // WL, features), BF16),
        scratch_shapes=[
            pltpu.VMEM((len(blocks), WL, size // WL, features), BF16),
            pltpu.SemaphoreType.DMA((len(blocks),)),
        ],
        compiler_params=pltpu.CompilerParams(vmem_limit_bytes=16 * MIB),
        cost_estimate=pl.CostEstimate(
            flops=0, bytes_accessed=4 * len(blocks) * size * features, transcendentals=0
        ),
    )(*flat)


def body(
    latent_state,
    obs_rows,
    obs_cells,
    obs_counts,
    w_obs,
    w_qkv,
    w_out,
    logit_scale,
    pos_bias,
    out_gain,
):
    levels, lat_cells, lon_cells, features = latent_state.shape
    lat_devices = lax.axis_size("lat")
    lon_devices = lax.axis_size("lon")
    devices = lat_devices * lon_devices
    both = ("lat", "lon")
    capacity = obs_rows.shape[2] // devices
    channels = obs_rows.shape[3]

    packed = pack(
        obs_rows.reshape(devices, capacity, channels),
        obs_cells.reshape(1, devices * capacity),
        obs_counts.reshape(1, devices),
    )
    packed = lax.all_to_all(packed, both, split_axis=0, concat_axis=0, tiled=True)
    base, folded, bias = project(
        latent_state.reshape(-1, features), w_obs, w_qkv, pos_bias, lon_cells
    )
    gain = out_gain[None]

    def attend(strip_at, carried=None):
        return attend_strip(
            strip_at, packed, logit_scale, gain, base, folded, bias, latent_state, w_obs, w_out, carried
        )

    south = [(i, i + 1) for i in range(lat_devices - 1)]
    east = [(i, (i + 1) % lon_devices) for i in range(lon_devices)]
    low_near, low_far, low_edge = attend(1)
    first = lax.ppermute(low_far, "lat", south)
    top_near, top_far, edges = attend(0, low_edge)
    edges = lax.ppermute(edges, "lon", east)
    first_edge = lax.ppermute(corner(first, lon_cells), "lon", east)
    joined = join(
        [
            (first, first_edge),
            (top_near, edges),
            (top_far, edges),
            (low_near, edges),
        ],
        lon_cells,
    )
    return joined.reshape(levels, lat_cells, lon_cells, features)


def solution(mesh):
    in_specs = (
        P(None, "lat", "lon", None),
        P("lat", "lon", None, None),
        P("lat", "lon", None),
        P("lat", "lon", None),
        P(),
        P(),
        P(),
        P(),
        P(),
        P(),
    )
    out_specs = P(None, "lat", "lon", None)
    return jax.shard_map(body, mesh=mesh, in_specs=in_specs, out_specs=out_specs, check_vma=False)
```

time: 66.7 us -> 71.8 us (1.076)
  local copies, waits for them, and re-layouts: 0.01 us -> 12.6 us
  Pallas kernels: 46.2 us -> 38.9 us
  starting transfers between devices: 11.9 us -> 11.1 us
    unnamed x2 -> x12, local copies, waits for them, and re-layouts: 0.01 us -> 12.6 us
    pallas_call x2, Pallas kernels: 20.1 us -> 15.5 us  [the longest x1 13.7 us: project(): pl.pallas_call(functools.partial(project_kernel, lon_cells), in_specs=[th...]
    pallas_call x2, Pallas kernels: 23.6 us -> 21.1 us  [attend_strip(): pl.pallas_call(functools.partial(strip_kernel, strip_at, lon_cells, passe...]
    ppermute x1, waiting for transfers between devices: 0.66 us -> 2.12 us  [body(): first = lax.ppermute(low_far, 'lat', south)]
    ppermute x1, starting transfers between devices: 0.96 us -> 0.06 us  [body(): first_edge = lax.ppermute(corner(first, lon_cells), 'lon', east)]
  transfers between devices with their start and end apart: 4 -> 4, of which waited for: 4 -> 3; matrix products, arithmetic and copies ran while one was open for 0% -> 0% of each run, Pallas kernels for 45% -> 34%
where the time goes in v2:
time: 71.8 us; the launch traced here: 71.5 us
  Pallas kernels  38.9 us (54%)
  local copies, waits for them, and re-layouts  12.6 us (18%)
  starting transfers between devices  11.1 us (15%)
  waiting for transfers between devices  8.7 us (12%)
    pallas_call x2, Pallas kernels, attend_strip(): pl.pallas_call(functools.partial(strip_kernel, strip_at, lon_cells, passe...  21.1 us
    pallas_call x1, Pallas kernels, project(): pl.pallas_call(functools.partial(project_kernel, lon_cells), in_specs=[th...  13.7 us
    unnamed x12, local copies, waits for them, and re-layouts  12.6 us
    all_to_all x1, starting transfers between devices, body(): lax.all_to_all(packed, both, split_axis=0, concat_axis=0, tiled=True)  7.3 us
    ppermute x1, waiting for transfers between devices, body(): edges = lax.ppermute(edges, 'lon', east)  5.51 us
    ppermute x1, starting transfers between devices, body(): first = lax.ppermute(low_far, 'lat', south)  3.71 us
    pallas_call x1, Pallas kernels, pack(): pl.pallas_call(pack_kernel, out_shape=jax.ShapeDtypeStruct((devices, held...  2.15 us
    ppermute x1, waiting for transfers between devices, body(): first = lax.ppermute(low_far, 'lat', south)  2.12 us
  transfers between devices with their start and end apart: 4, of which 3 were waited for; matrix products, arithmetic and copies ran while one was open for 0% of the time, Pallas kernels for 34%

profile of v2, /device:TPU:0, one launch (start us, length us, event | category | flops | bytes accessed | tf_op | source)
XLA Modules:
  0.0 71.5 jit_solution(1999669068795605158)
XLA Ops:
  0.0 2.2 %shard_map.100 = bf16[32,72,128]{2,1,0:T(8,128)(2,1)} custom-call(bf16[32,32,256]{2,1,0:T(8,128)(2,1)} %bitcast.8, s32[1,1024]{1,0:T(1,128)} %bitcast.9, s32[1,32]{1,0:T(1,128)} %bitcast.10), custom_call_target="tpu_custom_call" | custom-call | tf_op jit(solution)/shard_map/pallas_call | solution.py:89
  2.2 7.3 %all-to-all-start = ((bf16[32,72,128]{2,1,0:T(8,128)(2,1)}), bf16[32,72,128]{2,1,0:T(8,128)(2,1)S(1)}, u32[]{:S(2)}, u32[]{:S(2)}) async-start(bf16[32,72,128]{2,1,0:T(8,128)(2,1)} %shard_map.100), calls=%async_computation | async-start | bytes 1179648 | tf_op jit(solution)/shard_map/all_to_all | solution.py:526
  9.5 0.0 copy-start
  9.5 0.0 copy-start.1
  9.5 13.7 %shard_map.101 = (f32[12,1152,256]{2,1,0:T(8,128)S(1)}, bf16[12,256,256]{2,1,0:T(8,128)(2,1)S(1)}, f32[16,144,144]{2,1,0:T(8,128)S(1)}) custom-call(bf16[1152,1024]{1,0:T(8,128)(2,1)} %bitcast.11, bf16[256,1024]{1,0:T(8,128)(2,1)} %w_obs_hbm.5, bf16[1024,3072]{1,0:T(8,128)(2,1)} %w_hbm.1, f32[16,144,144]{2,1,0:T(8,128)} %bias_hbm.1), custom_call_target="tpu_custom_call" | custom-call | flops 8858370048 | bytes 25165824 | tf_op jit(solution)/shard_map/pallas_call | solution.py:176
  23.2 0.0 copy-start.2
  23.3 5.0 %copy-done.2 = f32[12,1152,256]{2,1,0:T(8,128)} copy-done((f32[12,1152,256]{2,1,0:T(8,128)}, f32[12,1152,256]{2,1,0:T(8,128)S(1)}, u32[]{:S(2)}) %copy-start.2) | copy-done | bytes 14155800
  28.3 0.0 copy-start.4
  28.3 1.1 %copy-done.4 = bf16[12,256,256]{2,1,0:T(8,128)(2,1)} copy-done((bf16[12,256,256]{2,1,0:T(8,128)(2,1)}, bf16[12,256,256]{2,1,0:T(8,128)(2,1)S(1)}, u32[]{:S(2)}) %copy-start.4) | copy-done | bytes 1572888
  29.4 0.0 all-to-all-done.packed_ref
  29.4 0.0 copy-done
  29.4 0.0 copy-done.1
  29.4 0.0 copy-start.3
  29.4 5.0 %copy-done.3 = f32[12,1152,256]{2,1,0:T(8,128)S(1)} copy-done((f32[12,1152,256]{2,1,0:T(8,128)S(1)}, f32[12,1152,256]{2,1,0:T(8,128)}, u32[]{:S(2)}) %copy-start.3) | copy-done | bytes 14155800
  34.5 0.0 copy-start.5
  34.5 1.4 %copy-done.5 = bf16[12,256,256]{2,1,0:T(8,128)(2,1)S(1)} copy-done((bf16[12,256,256]{2,1,0:T(8,128)(2,1)S(1)}, bf16[12,256,256]{2,1,0:T(8,128)(2,1)}, u32[]{:S(2)}) %copy-start.5) | copy-done | bytes 1572888
  35.9 10.4 %shard_map.102 = (bf16[288,1024]{1,0:T(8,128)(2,1)S(1)}, bf16[288,1024]{1,0:T(8,128)(2,1)S(1)}, bf16[48,1024]{1,0:T(8,128)(2,1)S(1)}) custom-call(bf16[32,72,128]{2,1,0:T(8,128)(2,1)S(1)} %all-to-all-done.packed_ref, f32[16]{0:T(128)S(1)} %copy-done.1, f32[1,1024]{1,0:T(1,128)S(1)} %bitcast.6, f32[12,1152,256]{2,1,0:T(8,128)S(1)} %copy-done.3, ...), custom_call_target="tpu_custom_call" | custom-call | flops 8455716864 | bytes 15466496 | tf_op jit(solution)/shard_map/pallas_call | solution.py:403
  46.3 3.7 %collective-permute-start = (bf16[288,1024]{1,0:T(8,128)(2,1)S(1)}, bf16[288,1024]{1,0:T(8,128)(2,1)S(1)}, u32[]{:S(2)}, u32[]{:S(2)}) collective-permute-start(bf16[288,1024]{1,0:T(8,128)(2,1)S(1)} %get-tuple-element.17), channel_id=1, source_target_pairs={{0,8},{8,16},{16,24},{1,9},{9,17},{17,25},{2,10},{10,18},{18,26},{... | collective-permute-start | bytes 1769480 | tf_op jit(solution)/shard_map/ppermute | solution.py:540
  50.0 10.7 %shard_map.104 = (bf16[288,1024]{1,0:T(8,128)(2,1)S(1)}, bf16[288,1024]{1,0:T(8,128)(2,1)S(1)}, bf16[144,1024]{1,0:T(8,128)(2,1)S(1)}) custom-call(bf16[32,72,128]{2,1,0:T(8,128)(2,1)S(1)} %all-to-all-done.packed_ref, f32[16]{0:T(128)S(1)} %copy-done.1, f32[1,1024]{1,0:T(1,128)S(1)} %bitcast.7, f32[12,1152,256]{2,1,0:T(8,128)S(1)} %copy-done.3, ...), custom_call_target="tpu_custom_call" | custom-call | flops 8455716864 | bytes 15466496 | tf_op jit(solution)/shard_map/pallas_call | solution.py:403
  60.7 0.1 collective-permute-start.2
  60.8 2.1 %collective-permute-done.block_ref.refs_0_ = bf16[288,1024]{1,0:T(8,128)(2,1)S(1)} collective-permute-done((bf16[288,1024]{1,0:T(8,128)(2,1)S(1)}, bf16[288,1024]{1,0:T(8,128)(2,1)S(1)}, u32[]{:S(2)}, u32[]{:S(2)}) %collective-permute-start) | collective-permute-done | bytes 589856 | tf_op jit(solution)/shard_map/ppermute | solution.py:540
  62.9 0.2 shard_map.103
  63.1 0.1 collective-permute-start.1
  63.2 5.5 %collective-permute-done.2.refs_3_.refs_5_.refs_7_ = bf16[144,1024]{1,0:T(8,128)(2,1)S(1)} collective-permute-done((bf16[144,1024]{1,0:T(8,128)(2,1)S(1)}, bf16[144,1024]{1,0:T(8,128)(2,1)S(1)}, u32[]{:S(2)}, u32[]{:S(2)}) %collective-permute-start.2) | collective-permute-done | bytes 294944 | tf_op jit(solution)/shard_map/ppermute | solution.py:542
  68.7 1.1 %collective-permute-done.1.refs_1_ = bf16[48,1024]{1,0:T(8,128)(2,1)S(1)} collective-permute-done((bf16[48,1024]{1,0:T(8,128)(2,1)S(1)}, bf16[48,1024]{1,0:T(8,128)(2,1)S(1)}, u32[]{:S(2)}, u32[]{:S(2)}) %collective-permute-start.1) | collective-permute-done | bytes 98336 | tf_op jit(solution)/shard_map/ppermute | solution.py:543
  69.7 1.7 %shard_map.105 = bf16[2,4,144,1024]{3,2,1,0:T(8,128)(2,1)} custom-call(bf16[288,1024]{1,0:T(8,128)(2,1)S(1)} %collective-permute-done.block_ref.refs_0_, bf16[48,1024]{1,0:T(8,128)(2,1)S(1)} %collective-permute-done.1.refs_1_, bf16[288,1024]{1,0:T(8,128)(2,1)S(1)} %get-tuple-element.19.refs_2_, ...), custom_call_target="tpu_custom_call" | custom-call | bytes 4718592 | tf_op jit(solution)/shard_map/pallas_call | solution.py:485
Async XLA Ops:
  2.2 27.3 %all-to-all-start = ((bf16[32,72,128]{2,1,0:T(8,128)(2,1)}), bf16[32,72,128]{2,1,0:T(8,128)(2,1)S(1)}, u32[]{:S(2)}, u32[]{:S(2)}) async-start(bf16[32,72,128]{2,1,0:T(8,128)(2,1)} %shard_map.100), calls=%async_computation | async-start | bytes 1179648 | tf_op jit(solution)/shard_map/all_to_all | solution.py:526
  9.5 20.0 %copy-start = (f32[1024]{0:T(1024)S(1)}, f32[1024]{0:T(1024)}, u32[]{:S(2)}) copy-start(f32[1024]{0:T(1024)} %param.19) | copy-start | bytes 12292
  9.5 20.0 %copy-start.1 = (f32[16]{0:T(128)S(1)}, f32[16]{0:T(128)}, u32[]{:S(2)}) copy-start(f32[16]{0:T(128)} %scale_ref.3) | copy-start | bytes 196
  23.2 5.0 %copy-start.2 = (f32[12,1152,256]{2,1,0:T(8,128)}, f32[12,1152,256]{2,1,0:T(8,128)S(1)}, u32[]{:S(2)}) copy-start(f32[12,1152,256]{2,1,0:T(8,128)S(1)} %get-tuple-element.14.base_ref) | copy-start | bytes 42467332
  28.3 1.1 %copy-start.4 = (bf16[12,256,256]{2,1,0:T(8,128)(2,1)}, bf16[12,256,256]{2,1,0:T(8,128)(2,1)S(1)}, u32[]{:S(2)}) copy-start(bf16[12,256,256]{2,1,0:T(8,128)(2,1)S(1)} %get-tuple-element.15.folded_ref) | copy-start | bytes 4718596
  29.4 5.0 %copy-start.3 = (f32[12,1152,256]{2,1,0:T(8,128)S(1)}, f32[12,1152,256]{2,1,0:T(8,128)}, u32[]{:S(2)}) copy-start(f32[12,1152,256]{2,1,0:T(8,128)} %copy-done.2) | copy-start | bytes 42467332
  34.5 1.4 %copy-start.5 = (bf16[12,256,256]{2,1,0:T(8,128)(2,1)S(1)}, bf16[12,256,256]{2,1,0:T(8,128)(2,1)}, u32[]{:S(2)}) copy-start(bf16[12,256,256]{2,1,0:T(8,128)(2,1)} %copy-done.4) | copy-start | bytes 4718596
  46.3 16.6 %collective-permute-start = (bf16[288,1024]{1,0:T(8,128)(2,1)S(1)}, bf16[288,1024]{1,0:T(8,128)(2,1)S(1)}, u32[]{:S(2)}, u32[]{:S(2)}) collective-permute-start(bf16[288,1024]{1,0:T(8,128)(2,1)S(1)} %get-tuple-element.17), channel_id=1, source_target_pairs={{0,8},{8,16},{16,24},{1,9},{9,17},{17,25},{2,10},{10,18},{18,26},{... | collective-permute-start | bytes 1769480 | tf_op jit(solution)/shard_map/ppermute | solution.py:540
  60.7 8.0 %collective-permute-start.2 = (bf16[144,1024]{1,0:T(8,128)(2,1)S(1)}, bf16[144,1024]{1,0:T(8,128)(2,1)S(1)}, u32[]{:S(2)}, u32[]{:S(2)}) collective-permute-start(bf16[144,1024]{1,0:T(8,128)(2,1)S(1)} %get-tuple-element.20), channel_id=1, source_target_pairs={{0,1},{1,2},{2,3},{3,4},{4,5},{5,6},{6,7},{7,0},{8,9},{9,10},{10,1... | collective-permute-start | bytes 884744 | tf_op jit(solution)/shard_map/ppermute | solution.py:542
  63.1 6.6 %collective-permute-start.1 = (bf16[48,1024]{1,0:T(8,128)(2,1)S(1)}, bf16[48,1024]{1,0:T(8,128)(2,1)S(1)}, u32[]{:S(2)}, u32[]{:S(2)}) collective-permute-start(bf16[48,1024]{1,0:T(8,128)(2,1)S(1)} %shard_map.103), channel_id=1, source_target_pairs={{0,1},{1,2},{2,3},{3,4},{4,5},{5,6},{6,7},{7,0},{8,9},{9,10},{10,1... | collective-permute-start | bytes 294920 | tf_op jit(solution)/shard_map/ppermute | solution.py:543
